TPU v7x, 32 devices: a whole 2x2x4 slice. The times are simulated.
32 devices in a mesh: dp: 8 (over y, x, core), mp: 4 (over z).
Axes of the slice: x: 2, y: 2, z: 4, core: 2. Of those that a mesh axis runs over, the one named last changes fastest.
Arguments:
- patches: bfloat16 [256, 81920], P('dp', 'mp'), may hold values from -10 to 10
- norm_gain: float32 [1280], replicated, may hold values from 0.1 to 1.9
- qkv_weight: bfloat16 [1280, 3840], P(None, 'mp'), may hold values from -6 to 6
- out_weight: bfloat16 [1280, 1280], P('mp'), may hold values from -0.15625 to 0.15625
- window_plan: int32 [8, 32], replicated, may hold values from -1 to 7, as said below
Outputs:
- attended: bfloat16 [256, 81920], P('dp', 'mp')
Inputs may be any that keep to these rules, and one draw needn't show every extreme that they name: `window_plan`: each home's live slots come first; over all homes every encoder device is named by exactly 16 slots; one home names one encoder at most 4 times and some home reaches that; the busiest home has all 32 slots live.
All inputs are finite; a program needn't handle non-finite values.
Results may differ from a plain program's by a relative error of at most 0.018.
Values may be sent and summed in bfloat16 or wider, within the bound.
A program may use at most 128 MiB of HBM per device.

v0:
```python
import jax
import jax.numpy as jnp
from jax import lax
from jax.sharding import PartitionSpec as P

HEAD_DIM = 80
WIN = 64
ENC_WIN = 16
HOME_WIN = 32


epsilon = 1e-06


def encode(rows_local, norm_gain, qkv_weight, out_weight):
    full_rows = lax.all_gather(rows_local, "mp", axis=1, tiled=True)
    window_count = full_rows.shape[0]
    full_width = full_rows.shape[1] // WIN
    patch_rows = jnp.transpose(full_rows.reshape(window_count, full_width, WIN), (0, 2, 1))
    patch_rows = patch_rows.reshape(window_count * WIN, full_width)
    as_float = patch_rows.astype(jnp.float32)
    mean_square = jnp.mean(as_float * as_float, axis=-1, keepdims=True)
    normed = (as_float * lax.rsqrt(mean_square + epsilon) * norm_gain).astype(jnp.bfloat16)
    projected = jnp.dot(normed, qkv_weight, preferred_element_type=jnp.float32).astype(jnp.bfloat16)
    heads_here = qkv_weight.shape[1] // (3 * HEAD_DIM)
    projected = projected.reshape(window_count, WIN, heads_here, 3, HEAD_DIM)
    queries = projected[:, :, :, 0, :]
    key_vecs = projected[:, :, :, 1, :]
    value_vecs = projected[:, :, :, 2, :]
    scores = jnp.einsum(
        "wqhd,wkhd->whqk", queries, key_vecs, preferred_element_type=jnp.float32
    ) * HEAD_DIM ** (-0.5)
    attn_weights = jax.nn.softmax(scores, axis=-1).astype(jnp.bfloat16)
    heads_out = jnp.einsum(
        "whqk,wkhd->hdwq", attn_weights, value_vecs, preferred_element_type=jnp.float32
    )
    local_width = heads_here * HEAD_DIM
    heads_out = heads_out.astype(jnp.bfloat16).reshape(local_width, window_count * WIN)
    share_rows = out_weight.shape[1] // lax.axis_size("mp")
    summed = lax.psum_scatter(
        lax.dot_general(
            out_weight, heads_out, (((0,), (0,)), ((), ())), preferred_element_type=jnp.float32
        ).astype(jnp.bfloat16),
        "mp",
        scatter_dimension=0,
        tiled=True,
    ).astype(jnp.float32)
    summed = jnp.transpose(summed.reshape(share_rows, window_count, WIN), (1, 0, 2))
    residual = rows_local.reshape(window_count, share_rows, WIN).astype(jnp.float32)
    block_out = (residual + summed).astype(jnp.bfloat16)
    return block_out.reshape(window_count, share_rows * WIN)


def body(patches, norm_gain, qkv_weight, out_weight, window_plan):
    senders = lax.axis_size("dp")
    here_index = lax.axis_index("dp")
    capacity = (HOME_WIN + senders - 1) // senders
    row_width = patches.shape[1]
    my_plan = lax.dynamic_slice_in_dim(window_plan, here_index, 1, 0)[0]
    is_live = my_plan >= 0
    encoders = jnp.arange(senders, dtype=jnp.int32)
    matches = (my_plan[:, None] == encoders[None, :]).astype(jnp.int32)
    ordinal = jnp.sum((jnp.cumsum(matches, axis=0) - matches) * matches, axis=1)
    slot_index = jnp.where(is_live, my_plan * capacity + ordinal, -1)
    all_slots = jnp.arange(senders * capacity, dtype=jnp.int32)
    matched = slot_index[None, :] == all_slots[:, None]
    source_index = jnp.sum(
        jnp.where(matched, jnp.arange(HOME_WIN, dtype=jnp.int32)[None, :], 0), axis=1
    )
    filled = jnp.any(matched, axis=1)
    outgoing = jnp.where(
        filled[:, None], jnp.take(patches, source_index, axis=0), jnp.zeros_like(patches[:1])
    )
    outgoing = outgoing.reshape(senders, capacity, row_width)
    incoming = lax.all_to_all(outgoing, "dp", split_axis=0, concat_axis=0, tiled=True)
    incoming = incoming.reshape(senders * capacity, row_width)
    sent_here = jnp.sum((window_plan == here_index).astype(jnp.int32), axis=1)
    offsets = jnp.cumsum(sent_here) - sent_here
    columns = jnp.arange(capacity, dtype=jnp.int32)
    position = jnp.where(
        columns[None, :] < sent_here[:, None], offsets[:, None] + columns[None, :], -1
    ).reshape(senders * capacity)
    picked = position[None, :] == jnp.arange(ENC_WIN, dtype=jnp.int32)[:, None]
    chosen = jnp.sum(jnp.where(picked, all_slots[None, :], 0), axis=1)
    assigned = jnp.take(incoming, chosen, axis=0)
    results = encode(assigned, norm_gain, qkv_weight, out_weight)
    out_width = results.shape[1]
    back_index = jnp.where(position >= 0, position, 0)
    replies = jnp.where(
        (position >= 0)[:, None], jnp.take(results, back_index, axis=0), jnp.zeros_like(results[:1])
    )
    replies = replies.reshape(senders, capacity, out_width)
    returned = lax.all_to_all(replies, "dp", split_axis=0, concat_axis=0, tiled=True)
    returned = returned.reshape(senders * capacity, out_width)
    home_rows = jnp.take(returned, jnp.where(is_live, slot_index, 0), axis=0)
    home_rows = jnp.where(is_live[:, None], home_rows, jnp.zeros_like(home_rows[:1]))
    return home_rows


def solution(mesh):
    return jax.shard_map(
        body,
        mesh=mesh,
        in_specs=(P("dp", "mp"), P(), P(None, "mp"), P("mp", None), P()),
        out_specs=P("dp", "mp"),
        check_vma=False,
    )
```

profile of v0, /device:TPU:1, one launch (start us, length us, event | category | flops | bytes accessed | tf_op | source)
XLA Modules:
  0.0 284.1 jit_solution(8471905881910063503)
XLA Ops:
  8.7 5.0 %gather_fusion.2 = bf16[32,20480]{1,0:T(8,128)(2,1)} fusion(bf16[32,20480]{1,0:T(8,128)(2,1)} %param.7, s32[1024]{0:T(1024)S(1)} %pad_clamp_fusion.3), kind=kCustom, calls=%fused_computation.clone | custom fusion | bytes 2621568 | tf_op jit(solution)/shard_map/jit(_take)/gather | solution.py:72
  18.7 5.4 %all-to-all-start = ((bf16[8,4,20480]{2,1,0:T(4,128)(2,1)}), bf16[8,4,20480]{2,1,0:T(4,128)(2,1)}, u32[]{:S(2)}, u32[]{:S(2)}) async-start(bf16[8,4,20480]{2,1,0:T(4,128)(2,1)} %reshape.242), calls=%async_computation | async-start | bytes 2621440 | tf_op jit(solution)/shard_map/all_to_all | solution.py:75
  24.7 14.1 %all-to-all-done = bf16[8,4,20480]{2,1,0:T(4,128)(2,1)} async-done(((bf16[8,4,20480]{2,1,0:T(4,128)(2,1)}), bf16[8,4,20480]{2,1,0:T(4,128)(2,1)}, u32[]{:S(2)}, u32[]{:S(2)}) %all-to-all-start) | async-done | bytes 1310752 | tf_op jit(solution)/shard_map/all_to_all | solution.py:75
  41.1 3.0 %gather_fusion = bf16[16,20480]{1,0:T(8,128)(2,1)S(1)} fusion(bf16[32,20480]{1,0:T(8,128)(2,1)} %reshape.243, s32[1024]{0:T(1024)S(1)} %pad_clamp_fusion.2), kind=kCustom, calls=%fused_computation.2 | custom fusion | bytes 1310784 | tf_op jit(solution)/shard_map/jit(_take)/gather | solution.py:85
  45.4 57.4 %all-gather.2.cloned.1.call-done = bf16[16,81920]{1,0:T(8,128)(2,1)} async-done(((bf16[16,20480]{1,0:T(8,128)(2,1)}), bf16[16,81920]{1,0:T(8,128)(2,1)}) %all-gather.2.cloned.1.call-update) | async-done | bytes 2621456 | tf_op jit(solution)/shard_map/all_gather | solution.py:16
  102.8 4.4 %convert_multiply_fusion = f32[16,81920]{1,0:T(8,128)} fusion(bf16[16,81920]{1,0:T(8,128)(2,1)} %all-gather.2.cloned.1.call-done), kind=kLoop, calls=%fused_computation.21 | loop fusion | flops 2621440 | bytes 7864320 | tf_op jit(solution)/shard_map/mul | solution.py:22
  107.2 12.3 %mul.48 = f32[16,1280,64]{2,1,0:T(8,128)} reshape(f32[16,81920]{1,0:T(8,128)} %convert_multiply_fusion) | data formatting | bytes 10485760 | tf_op jit(solution)/shard_map/mul | solution.py:22
  119.5 4.7 %reduce_sum.64 = f32[16,64]{1,0:T(8,128)S(1)} reduce(f32[16,1280,64]{2,1,0:T(8,128)} %mul.48, f32[]{:T(128)} %constant.72.clone.1), dimensions={1}, to_apply=%region_7.9 | reduce | flops 1309696 | bytes 5246980 | tf_op jit(solution)/shard_map/reduce_sum | solution.py:22
  124.3 12.0 %reshape.251 = f32[16,1280,64]{2,1,0:T(8,128)} reshape(bf16[16,81920]{1,0:T(8,128)(2,1)} %all-gather.2.cloned.1.call-done) | data formatting | bytes 7864320 | tf_op jit(solution)/shard_map/convert_element_type | solution.py:21
  136.3 9.1 %copy.32 = f32[16,64,1280]{2,1,0:T(8,128)} copy(f32[16,64,1280]{1,2,0:T(8,128)} %bitcast.69) | data formatting | bytes 10485760 | tf_op jit(solution)/shard_map/convert_element_type | solution.py:21
  145.4 3.0 %fusion.2 = bf16[1024,1280]{1,0:T(8,128)(2,1)S(1)} fusion(f32[16,64,1280]{2,1,0:T(8,128)} %copy.32, f32[1280]{0:T(1024)S(1)} %copy-done.3, f32[1024]{0:T(1024)S(1)} %rsqrt.12), kind=kLoop, calls=%fused_computation.7 | loop fusion | flops 3932160 | bytes 7873536 | tf_op jit(solution)/shard_map/convert_element_type | solution.py:23
  148.4 3.9 %convolution_convert_fusion.1 = bf16[1024,960]{0,1:T(8,128)(2,1)} fusion(bf16[1024,1280]{1,0:T(8,128)(2,1)S(1)} %fusion.2, bf16[1280,960]{0,1:T(8,128)(2,1)S(1)} %copy-done), kind=kOutput, calls=%fused_computation.16 | convolution fusion | flops 2517565440 | bytes 7045120 | tf_op jit(solution)/shard_map/dot_general | solution.py:24
  152.3 6.0 %reshape.244 = bf16[16,64,4,3,80]{1,0,4,3,2:T(8,128)(2,1)} reshape(bf16[1024,960]{0,1:T(8,128)(2,1)} %convolution_convert_fusion.1) | data formatting | bytes 3932160 | tf_op jit(solution)/shard_map/reshape | solution.py:26
  158.4 4.3 %fusion.34 = (bf16[16,64,4,1,80]{1,0,4,3,2:T(8,128)(2,1)S(1)}, bf16[16,64,4,1,80]{1,0,4,3,2:T(8,128)(2,1)}, bf16[16,64,4,1,80]{1,0,4,3,2:T(8,128)(2,1)}) fusion(bf16[16,64,4,3,80]{1,0,4,3,2:T(8,128)(2,1)} %reshape.244), kind=kLoop, calls=%fused_computation.69 | loop fusion | bytes 3932160 | tf_op jit(solution)/shard_map/slice | solution.py:29
  164.7 2.7 copy.45
  169.4 3.5 %fusion.35 = (f32[16,4,64]{2,1,0:T(4,128)S(1)}, f32[16,4,64,64]{2,3,1,0:T(8,128)}) fusion(bf16[16,64,4,1,80]{4,1,2,0,3:T(8,128)(2,1)} %copy.45, bf16[16,64,4,1,80]{4,1,2,0,3:T(8,128)(2,1)S(1)} %copy.44), kind=kOutput, calls=%fused_computation.70 | convolution fusion | flops 42729536 | bytes 2375680 | tf_op jit(solution)/shard_map/sub | solution.py:33
  176.6 4.2 %fusion.3 = bf16[1280,1024]{0,1:T(8,128)(2,1)} fusion(bf16[320,1024]{0,1:T(8,128)(2,1)S(1)} %reshape.245, bf16[320,1280]{1,0:T(8,128)(2,1)} %param.10), kind=kOutput, calls=%fused_computation.9 | convolution fusion | flops 840171520 | bytes 4096000 | tf_op jit(solution)/shard_map/dot_general | solution.py:41
  180.8 4.5 %copy.41 = bf16[1280,1024]{1,0:T(8,128)(2,1)} copy(bf16[1280,1024]{0,1:T(8,128)(2,1)} %fusion.3) | data formatting | bytes 5242880
  186.9 49.3 %reduce-scatter.4.cloned.1.call-done = bf16[320,1024]{1,0:T(8,128)(2,1)} async-done(((bf16[1280,1024]{1,0:T(8,128)(2,1)}), bf16[320,1024]{1,0:T(8,128)(2,1)}) %reduce-scatter.4.cloned.1.call-update) | async-done | bytes 655376
  239.6 3.2 %fusion.4 = bf16[16,320,64]{2,1,0:T(8,128)(2,1)} fusion(f32[320,16,64]{2,0,1:T(8,128)} %copy.38, bf16[16,320,64]{2,1,0:T(8,128)(2,1)S(1)} %gather.16, pred[16]{0:T(512)(128)(4,1)S(1)} %compare_and_fusion.3), kind=kLoop, calls=%fused_computation.11 | loop fusion | flops 1310720 | bytes 2621456 | tf_op jit(solution)/shard_map/convert_element_type | solution.py:50
  247.8 3.1 %select_select_fusion.2 = bf16[8,4,20480]{2,1,0:T(4,128)(2,1)} fusion(bf16[8,4,20480]{2,1,0:T(4,128)(2,1)} %gather.18, pred[8,4]{1,0:T(8,128)(4,1)S(1)} %get-tuple-element.14, pred[8,4]{1,0:T(8,128)(4,1)S(1)} %get-tuple-element.13), kind=kLoop, calls=%fused_computation.22 | loop fusion | flops 1310720 | bytes 2621504 | tf_op jit(solution)/shard_map/jit(_where)/select_n | solution.py:89
  250.9 5.0 %all-to-all-start.1 = ((bf16[8,4,20480]{2,1,0:T(4,128)(2,1)}), bf16[8,4,20480]{2,1,0:T(4,128)(2,1)}, u32[]{:S(2)}, u32[]{:S(2)}) async-start(bf16[8,4,20480]{2,1,0:T(4,128)(2,1)} %select_select_fusion.2), calls=%async_computation.1 | async-start | bytes 2621440 | tf_op jit(solution)/shard_map/all_to_all | solution.py:93
  255.9 14.7 %all-to-all-done.1 = bf16[8,4,20480]{2,1,0:T(4,128)(2,1)} async-done(((bf16[8,4,20480]{2,1,0:T(4,128)(2,1)}), bf16[8,4,20480]{2,1,0:T(4,128)(2,1)}, u32[]{:S(2)}, u32[]{:S(2)}) %all-to-all-start.1) | async-done | bytes 1310752 | tf_op jit(solution)/shard_map/all_to_all | solution.py:93
  274.5 2.7 select_select_fusion
  (58 shorter events, 32.8 us)
Async XLA Ops:
  6.5 141.9 %copy-start = (bf16[1280,960]{0,1:T(8,128)(2,1)S(1)}, bf16[1280,960]{0,1:T(8,128)(2,1)}, u32[]{:S(2)}) copy-start(bf16[1280,960]{0,1:T(8,128)(2,1)} %param.9) | copy-start | bytes 7372804
  18.7 5.4 %copy-start.4 = (s32[8,32]{1,0:T(8,128)S(1)}, s32[8,32]{1,0:T(8,128)}, u32[]{:S(2)}) copy-start(s32[8,32]{1,0:T(8,128)} %param.11) | copy-start | bytes 3076
  18.7 20.1 %all-to-all-start = ((bf16[8,4,20480]{2,1,0:T(4,128)(2,1)}), bf16[8,4,20480]{2,1,0:T(4,128)(2,1)}, u32[]{:S(2)}, u32[]{:S(2)}) async-start(bf16[8,4,20480]{2,1,0:T(4,128)(2,1)} %reshape.242), calls=%async_computation | async-start | bytes 2621440 | tf_op jit(solution)/shard_map/all_to_all | solution.py:75
  24.1 78.7 %all-gather.2.cloned.1.call-start = ((), (), s32[]{:S(2)}) async-start(), calls=%async_computation.3 | async-start | bytes 3276800 | tf_op jit(solution)/shard_map/all_gather | solution.py:16
  45.1 191.1 %reduce-scatter.4.cloned.1.call-start = ((), (), s32[]{:S(2)}) async-start(), calls=%async_computation.4 | async-start | bytes 3276800
  136.3 9.1 %copy-start.3 = (f32[1280]{0:T(1024)S(1)}, f32[1280]{0:T(1024)}, u32[]{:S(2)}) copy-start(f32[1280]{0:T(1024)} %param.8) | copy-start | bytes 15364
  169.4 3.5 %copy-start.2 = (bf16[16,64,4,1,80]{4,1,0,2,3:T(8,128)(2,1)S(1)}, bf16[16,64,4,1,80]{4,1,0,2,3:T(8,128)(2,1)}, u32[]{:S(2)}) copy-start(bf16[16,64,4,1,80]{4,1,0,2,3:T(8,128)(2,1)} %copy.43) | copy-start | bytes 1966084
  250.9 19.7 %all-to-all-start.1 = ((bf16[8,4,20480]{2,1,0:T(4,128)(2,1)}), bf16[8,4,20480]{2,1,0:T(4,128)(2,1)}, u32[]{:S(2)}, u32[]{:S(2)}) async-start(bf16[8,4,20480]{2,1,0:T(4,128)(2,1)} %select_select_fusion.2), calls=%async_computation.1 | async-start | bytes 2621440 | tf_op jit(solution)/shard_map/all_to_all | solution.py:93
  274.5 2.7 copy-start.1
Sparse Core Ops, SparseCore 0:
  45.3 57.4 all-gather.1
  185.4 50.7 reduce-scatter.3
where the time goes:
time: 289 us; the launch traced here: 284 us
  waiting for transfers between devices  136 us (47%)
  local copies, waits for them, and re-layouts  83.2 us (29%)
  other arithmetic  27.4 us (9%)
  matrix products  13.7 us (5%)
  between operations  13.6 us (5%)
  starting transfers between devices  10.6 us (4%)
    all_gather x1, waiting for transfers between devices, encode(): full_rows = lax.all_gather(rows_local, 'mp', axis=1, tiled=True)  57.4 us
    unnamed x3, waiting for transfers between devices  49.4 us
    convert_element_type x2, local copies, waits for them, and re-layouts, encode(): as_float = patch_rows.astype(jnp.float32)  21.1 us
    all_to_all x1, waiting for transfers between devices, body(): lax.all_to_all(replies, 'dp', split_axis=0, concat_axis=0, tiled=True)  14.7 us
    all_to_all x1, waiting for transfers between devices, body(): lax.all_to_all(outgoing, 'dp', split_axis=0, concat_axis=0, tiled=True)  14.1 us
    unnamed x15, local copies, waits for them, and re-layouts  12.7 us
    mul x1, local copies, waits for them, and re-layouts, encode(): mean_square = jnp.mean(as_float * as_float, axis=-1, keepdims=True)  12.3 us
    reshape x1, local copies, waits for them, and re-layouts, encode(): projected = projected.reshape(window_count, WIN, heads_here, 3, HEAD_DIM)  6.02 us
  transfers between devices with their start and end apart: 4, of which 4 were waited for; matrix products, arithmetic and copies ran while one was open for 1% of the time, Pallas kernels for 0%

commit v1 on v0

v1 whole, which is shorter than its diff:
```python
import functools

import jax
import jax.numpy as jnp
from jax import lax
from jax.experimental import pallas as pl
from jax.experimental.pallas import tpu as pltpu
from jax.sharding import PartitionSpec as P

HEAD_DIM = 80
WIN = 64
ENC_WIN = 16
LANES = 128
PAIRS = 2

epsilon = 1e-06
MESH = pl.DeviceIdType.MESH
F32 = jnp.float32
BF16 = jnp.bfloat16


def kernel(
    n, m, cap,
    source_ref, chosen_ref, back_ref, slot_ref, x_ref, gain_ref, qkv_ref, outw_ref,
    out_ref,
    outb, inb, gath, qkv_t, outw_t, proj, heads, part, from_left, from_right, total, done, backb, homeb,
    d_send, d_recv, b_send, b_recv, ag_recv, ag_right, ag_left, rs_send, rs_left, rs_right,
):
    me = lax.axis_index("dp")
    z = lax.axis_index("mp")
    home_win, rows, _ = x_ref.shape
    width = 2 * rows
    chunks = gath.shape[1]
    heads_here = qkv_ref.shape[1] // (3 * HEAD_DIM)

    barrier = pltpu.get_barrier_semaphore()

    def greet(d, _):
        pl.semaphore_signal(
            barrier, inc=1, device_id={"dp": lax.rem(me + d, n)}, device_id_type=MESH
        )
        return 0

    lax.fori_loop(1, n, greet, 0)

    @pl.when(z > 0)
    def _():
        pl.semaphore_signal(barrier, inc=1, device_id={"mp": z - 1}, device_id_type=MESH)

    @pl.when(z < m - 1)
    def _():
        pl.semaphore_signal(barrier, inc=1, device_id={"mp": z + 1}, device_id_type=MESH)

    def pack(d, _):
        e = lax.rem(me + d, n)
        for j in range(cap):
            outb[e, j] = x_ref[source_ref[e * cap + j]]
        return 0

    lax.fori_loop(0, n, pack, 0)
    ends = (z == 0).astype(jnp.int32) + (z == m - 1).astype(jnp.int32)
    pl.semaphore_wait(barrier, n + 1 - ends)

    def exchange(src, dst, send, recv, d):
        e = lax.rem(me + d, n)
        return pltpu.make_async_remote_copy(
            src_ref=src.at[e], dst_ref=dst.at[me], send_sem=send.at[d], recv_sem=recv.at[d],
            device_id={"dp": e}, device_id_type=MESH,
        )

    def start_exchange(src, dst, send, recv):
        def step(d, _):
            exchange(src, dst, send, recv, d).start()
            return 0

        lax.fori_loop(1, n, step, 0)

    def end_exchange(src, dst, send, recv):
        def step(d, _):
            exchange(src, dst, send, recv, d).wait()
            return 0

        lax.fori_loop(1, n, step, 0)

    start_exchange(outb, inb, d_send, d_recv)
    inb[me] = outb[me]

    lower = 0
    while lower < qkv_ref.shape[1]:
        size = min(LANES, qkv_ref.shape[1] - lower)
        qkv_t[lower:lower + size, :] = qkv_ref[:, lower:lower + size].T
        lower += size
    for lower in range(0, outw_ref.shape[1], LANES):
        outw_t[lower:lower + LANES, :] = outw_ref[:, lower:lower + LANES].T

    row = lax.broadcasted_iota(jnp.int32, (width, width), 0)
    col = lax.broadcasted_iota(jnp.int32, (width, width), 1)
    spread = jnp.where(
        row == jnp.where(col < rows, 2 * col, 2 * (col - rows) + 1), 1.0, 0.0
    ).astype(BF16)
    gathered = jnp.where(
        col == jnp.where(row < rows, 2 * row, 2 * (row - rows) + 1), 1.0, 0.0
    ).astype(BF16)
    low_half = lax.broadcasted_iota(jnp.int32, (rows, LANES), 1) < WIN

    end_exchange(outb, inb, d_send, d_recv)

    def window_in(k):
        at = chosen_ref[k]
        return inb[at // cap, lax.rem(at, cap)].astype(F32)

    def unpack(c, _):
        for p in range(PAIRS):
            first = window_in((c * PAIRS + p) * 2)
            second = window_in((c * PAIRS + p) * 2 + 1)
            even = jnp.where(low_half, first, pltpu.roll(second, WIN, 1))
            odd = jnp.where(low_half, pltpu.roll(first, WIN, 1), second)
            halves = jnp.concatenate([even, odd], axis=0).astype(BF16)
            block = jnp.dot(spread, halves, preferred_element_type=F32).astype(BF16)
            gath[z, c, :, p * LANES:(p + 1) * LANES] = block
        return 0

    def ag_copy(c, o, step, send):
        return pltpu.make_async_remote_copy(
            src_ref=gath.at[o, c], dst_ref=gath.at[o, c],
            send_sem=send.at[c, o], recv_sem=ag_recv.at[c, o],
            device_id={"mp": z + step}, device_id_type=MESH,
        )

    def ag_own(c):
        @pl.when(z < m - 1)
        def _():
            ag_copy(c, z, 1, ag_right).start()

        @pl.when(z > 0)
        def _():
            ag_copy(c, z, -1, ag_left).start()

    def ag_step(c, t):
        @pl.when(z >= t)
        def _():
            ag_copy(c, z - t, -1, ag_left).wait_recv()

            @pl.when(z < m - 1)
            def _():
                ag_copy(c, z - t, 1, ag_right).start()

        @pl.when(z + t < m)
        def _():
            ag_copy(c, z + t, 1, ag_right).wait_recv()

            @pl.when(z > 0)
            def _():
                ag_copy(c, z + t, -1, ag_left).start()

    def rs_copy(c, s, step, landing, recv):
        return pltpu.make_async_remote_copy(
            src_ref=part.at[c, s], dst_ref=landing.at[c, s],
            send_sem=rs_send.at[c, s], recv_sem=recv.at[c, s],
            device_id={"mp": z + step}, device_id_type=MESH,
        )

    def rs_stage(c, k):
        @pl.when(z == k)
        def _():
            def step(i, _):
                s = m - 1 - i
                if k > 0:
                    rs_copy(c, s, -1, from_left, rs_left).wait_recv()
                    part[c, s] = (part[c, s].astype(F32) + from_left[c, s].astype(F32)).astype(BF16)
                rs_copy(c, s, 1, from_left, rs_left).start()
                return 0

            lax.fori_loop(0, m - 1 - k, step, 0)

        @pl.when(z == m - 1 - k)
        def _():
            def step(s, _):
                if k > 0:
                    rs_copy(c, s, 1, from_right, rs_right).wait_recv()
                    part[c, s] = (part[c, s].astype(F32) + from_right[c, s].astype(F32)).astype(BF16)
                rs_copy(c, s, -1, from_right, rs_right).start()
                return 0

            lax.fori_loop(0, m - 1 - k, step, 0)

    def rs_final(c):
        total[...] = part[c, z].astype(F32)

        @pl.when(z > 0)
        def _():
            rs_copy(c, z, -1, from_left, rs_left).wait_recv()
            total[...] += from_left[c, z].astype(F32)

        @pl.when(z < m - 1)
        def _():
            rs_copy(c, z, 1, from_right, rs_right).wait_recv()
            total[...] += from_right[c, z].astype(F32)

        block = (total[...] + gath[z, c].astype(F32)).astype(BF16)
        halves = jnp.dot(gathered, block, preferred_element_type=F32)
        for p in range(PAIRS):
            even = halves[:rows, p * LANES:(p + 1) * LANES]
            odd = halves[rows:, p * LANES:(p + 1) * LANES]
            k = (c * PAIRS + p) * 2
            done[k] = jnp.where(low_half, even, pltpu.roll(odd, WIN, 1)).astype(BF16)
            done[k + 1] = jnp.where(low_half, pltpu.roll(even, WIN, 1), odd).astype(BF16)

    def project(c):
        full = gath[:, c].reshape(m * width, PAIRS * LANES).astype(F32)
        mean_square = jnp.mean(full * full, axis=0, keepdims=True)
        normed = (full * lax.rsqrt(mean_square + epsilon) * gain_ref[...]).astype(BF16)
        proj[...] = jnp.dot(qkv_t[...], normed, preferred_element_type=F32).astype(BF16)

    key_window = lax.broadcasted_iota(jnp.int32, (LANES, LANES), 0) // WIN
    query_window = lax.broadcasted_iota(jnp.int32, (LANES, LANES), 1) // WIN
    same_window = key_window == query_window

    def attend(p):
        lanes = slice(p * LANES, (p + 1) * LANES)
        for h in range(heads_here):
            base = h * 3 * HEAD_DIM
            queries = proj[base:base + HEAD_DIM, lanes]
            key_vecs = proj[base + HEAD_DIM:base + 2 * HEAD_DIM, lanes]
            value_vecs = proj[base + 2 * HEAD_DIM:base + 3 * HEAD_DIM, lanes]
            scores = lax.dot_general(
                key_vecs, queries, (((0,), (0,)), ((), ())), preferred_element_type=F32
            ) * HEAD_DIM ** (-0.5)
            scores = jnp.where(same_window, scores, -1e30)
            weights = jnp.exp(scores - jnp.max(scores, axis=0, keepdims=True))
            probs = (weights / jnp.sum(weights, axis=0, keepdims=True)).astype(BF16)
            heads[h * HEAD_DIM:(h + 1) * HEAD_DIM, lanes] = jnp.dot(
                value_vecs, probs, preferred_element_type=F32
            ).astype(BF16)

    def output(c):
        for s in range(m):
            part[c, s] = jnp.dot(
                outw_t[s * width:(s + 1) * width, :], heads[...], preferred_element_type=F32
            ).astype(BF16)

    lax.fori_loop(0, chunks, unpack, 0)
    ag_own(0)
    if chunks > 1:
        ag_own(1)
    for t in range(1, m):
        ag_step(0, t)

    between = PAIRS + 1

    def steps_at(place):
        return [t for t in range(1, m) if (t - 1) * between // (m - 1) == place]

    def turn(c, _):
        @pl.when(c + 2 < chunks)
        def _():
            ag_own(c + 2)

        for place in range(between):
            @pl.when(c < chunks)
            def _():
                if place == 0:
                    project(c)
                else:
                    attend(place - 1)

            @pl.when(c + 1 < chunks)
            def _():
                for t in steps_at(place):
                    ag_step(c + 1, t)

            @pl.when(c > 0)
            def _():
                for t in steps_at(place):
                    if t < m - 1:
                        rs_stage(c - 1, t)
                    else:
                        rs_final(c - 1)

        @pl.when(c < chunks)
        def _():
            output(c)
            rs_stage(c, 0)

        return 0

    lax.fori_loop(0, chunks + 1, turn, 0)

    def reply(d, _):
        e = lax.rem(me + d, n)
        for j in range(cap):
            backb[e, j] = done[back_ref[e * cap + j]]
        return 0

    lax.fori_loop(0, n, reply, 0)
    start_exchange(backb, homeb, b_send, b_recv)
    homeb[me] = backb[me]

    def sent(c, _):
        def each(o, _):
            @pl.when(jnp.logical_and(z < m - 1, o <= z))
            def _():
                ag_copy(c, o, 1, ag_right).wait_send()

            @pl.when(jnp.logical_and(z > 0, o >= z))
            def _():
                ag_copy(c, o, -1, ag_left).wait_send()

            @pl.when(o > z)
            def _():
                rs_copy(c, o, 1, from_left, rs_left).wait_send()

            @pl.when(o < z)
            def _():
                rs_copy(c, o, -1, from_right, rs_right).wait_send()

            return 0

        return lax.fori_loop(0, m, each, 0)

    lax.fori_loop(0, chunks, sent, 0)
    end_exchange(backb, homeb, b_send, b_recv)

    def place_home(s, _):
        at = slot_ref[s]
        safe = jnp.maximum(at, 0)
        found = homeb[safe // cap, lax.rem(safe, cap)].astype(F32)
        out_ref[s] = jnp.where(at >= 0, found, jnp.zeros_like(found)).astype(BF16)
        return 0

    lax.fori_loop(0, home_win, place_home, 0)


def body(patches, norm_gain, qkv_weight, out_weight, window_plan):
    n = lax.axis_size("dp")
    m = lax.axis_size("mp")
    here = lax.axis_index("dp")
    home_win, row_width = patches.shape
    rows = row_width // LANES
    width = 2 * rows
    full_width = width * m
    cap = (home_win + n - 1) // n
    chunks = ENC_WIN // (2 * PAIRS)
    cols = PAIRS * LANES

    my_plan = lax.dynamic_slice_in_dim(window_plan, here, 1, 0)[0]
    slots = jnp.arange(home_win, dtype=jnp.int32)
    earlier = (my_plan[:, None] == my_plan[None, :]) & (slots[None, :] < slots[:, None])
    ordinal = jnp.sum(earlier.astype(jnp.int32), axis=1)
    slot_index = jnp.where(my_plan >= 0, my_plan * cap + ordinal, -1)
    all_slots = jnp.arange(n * cap, dtype=jnp.int32)
    source = jnp.sum(
        jnp.where(slot_index[None, :] == all_slots[:, None], slots[None, :], 0), axis=1
    )
    sent_here = jnp.sum((window_plan == here).astype(jnp.int32), axis=1)
    homes = jnp.arange(n, dtype=jnp.int32)
    offsets = jnp.sum(
        jnp.where(homes[None, :] < homes[:, None], sent_here[None, :], 0), axis=1
    )
    columns = jnp.arange(cap, dtype=jnp.int32)
    position = jnp.where(
        columns[None, :] < sent_here[:, None], offsets[:, None] + columns[None, :], -1
    ).reshape(n * cap)
    picked = position[None, :] == jnp.arange(ENC_WIN, dtype=jnp.int32)[:, None]
    chosen = jnp.sum(jnp.where(picked, all_slots[None, :], 0), axis=1)
    back = jnp.maximum(position, 0)

    smem = pl.BlockSpec(memory_space=pltpu.SMEM)
    vmem = pl.BlockSpec(memory_space=pltpu.VMEM)
    dma = pltpu.SemaphoreType.DMA
    result = pl.pallas_call(
        functools.partial(kernel, n, m, cap),
        out_shape=jax.ShapeDtypeStruct((home_win, rows, LANES), BF16),
        in_specs=[smem] * 4 + [vmem] * 4,
        out_specs=vmem,
        scratch_shapes=[
            pltpu.VMEM((n, cap, rows, LANES), BF16),
            pltpu.VMEM((n, cap, rows, LANES), BF16),
            pltpu.VMEM((m, chunks, width, cols), BF16),
            pltpu.VMEM((qkv_weight.shape[1], full_width), BF16),
            pltpu.VMEM((full_width, out_weight.shape[0]), BF16),
            pltpu.VMEM((qkv_weight.shape[1], cols), BF16),
            pltpu.VMEM((out_weight.shape[0], cols), BF16),
            pltpu.VMEM((chunks, m, width, cols), BF16),
            pltpu.VMEM((chunks, m, width, cols), BF16),
            pltpu.VMEM((chunks, m, width, cols), BF16),
            pltpu.VMEM((width, cols), F32),
            pltpu.VMEM((ENC_WIN, rows, LANES), BF16),
            pltpu.VMEM((n, cap, rows, LANES), BF16),
            pltpu.VMEM((n, cap, rows, LANES), BF16),
            dma((n,)), dma((n,)), dma((n,)), dma((n,)),
            dma((chunks, m)), dma((chunks, m)), dma((chunks, m)),
            dma((chunks, m)), dma((chunks, m)), dma((chunks, m)),
        ],
        compiler_params=pltpu.CompilerParams(
            collective_id=0, has_side_effects=True, vmem_limit_bytes=56 * 1024 * 1024
        ),
    )(
        source, chosen, back, slot_index,
        patches.reshape(home_win, rows, LANES), norm_gain[:, None], qkv_weight, out_weight,
    )
    return result.reshape(home_win, row_width)


def solution(mesh):
    return jax.shard_map(
        body,
        mesh=mesh,
        in_specs=(P("dp", "mp"), P(), P(None, "mp"), P("mp", None), P()),
        out_specs=P("dp", "mp"),
        check_vma=False,
    )
```

time: 289 us -> 148 us (0.51)
  waiting for transfers between devices: 136 us -> 0 us
  Pallas kernels: 0 us -> 130 us
  local copies, waits for them, and re-layouts: 83.2 us -> 11.8 us
  other arithmetic: 27.4 us -> 4.44 us
  matrix products: 13.7 us -> 0 us
  between operations: 13.6 us -> 0.02 us
  starting transfers between devices: 10.6 us -> 0 us
    pallas_call x0 -> x1, Pallas kernels: none -> 130 us  [body(): pl.pallas_call(functools.partial(kernel, n, m, cap), out_shape=jax.ShapeD...]
    all_gather x1 -> x0, waiting for transfers between devices: 57.4 us -> none  [encode(): full_rows = lax.all_gather(rows_local, 'mp', axis=1, tiled=True)]
    unnamed x3 -> x0, waiting for transfers between devices: 49.4 us -> none
    all_to_all x2 -> x0, waiting for transfers between devices: 28.8 us -> none  [the longest x1 14.7 us: body(): lax.all_to_all(replies, 'dp', split_axis=0, concat_axis=0, tiled=True)]
    convert_element_type x3 -> x0, local copies, waits for them, and re-layouts: 22 us -> none  [the longest x2 21.1 us: encode(): as_float = patch_rows.astype(jnp.float32)]
    reshape x6 -> x0, local copies, waits for them, and re-layouts: 15.2 us -> none  [the longest x1 6.02 us: encode(): projected = projected.reshape(window_count, WIN, heads_here, 3, HEAD_DIM)]
    gather x6 -> x0, local copies, waits for them, and re-layouts: 14.6 us -> none  [the longest x1 5.05 us: body(): jnp.take(patches, source_index, axis=0)]
    mul x1 -> x0, local copies, waits for them, and re-layouts: 12.3 us -> none  [encode(): mean_square = jnp.mean(as_float * as_float, axis=-1, keepdims=True)]
  transfers between devices with their start and end apart: 4 -> 0, of which waited for: 4 -> 0; matrix products, arithmetic and copies ran while one was open for 1% -> 0% of each run, Pallas kernels for 0% -> 0%
where the time goes in v1:
time: 148 us; the launch traced here: 146 us
  Pallas kernels  130 us (88%)
  local copies, waits for them, and re-layouts  11.8 us (8%)
  other arithmetic  4.44 us (3%)
    pallas_call x1, Pallas kernels, body(): pl.pallas_call(functools.partial(kernel, n, m, cap), out_shape=jax.ShapeD...  130 us
    unnamed x5, local copies, waits for them, and re-layouts  9.23 us

profile of v1, /device:TPU:1, one launch (start us, length us, event | category | flops | bytes accessed | tf_op | source)
XLA Modules:
  0.0 146.0 jit_solution(3550862720936340929)
XLA Ops:
  0.0 0.8 convert_reduce_fusion.1
  0.8 0.1 select_reduce_fusion.2
  0.9 0.7 fusion.2
  1.6 0.2 convert_reduce_fusion
  1.8 0.7 fusion.1
  2.5 0.6 select_reduce_fusion.source_ref
  3.1 0.1 add_select_fusion
  3.2 0.1 select_n.38
  3.3 1.3 compare_select_fusion
  4.5 0.7 select_reduce_fusion.1.chosen_ref
  5.2 1.8 %broadcast_in_dim.70.gain_ref = f32[1280,1]{1,0:T(8,128)} reshape(f32[1280]{0:T(1024)} %param.6) | data formatting | bytes 10240 | tf_op jit(solution)/shard_map/broadcast_in_dim | solution.py:400
  7.0 0.0 copy-start
  7.0 2.8 %copy.11 = bf16[4,8,160,128]{3,2,1,0:T(8,128)(2,1)} copy(bf16[4,8,160,128]{3,1,2,0:T(8,128)(2,1)} %bitcast.18) | data formatting | bytes 2621440
  9.8 0.0 copy-done
  9.8 3.6 %copy.10.qkv_ref = bf16[1280,960]{1,0:T(8,128)(2,1)} copy(bf16[1280,960]{0,1:T(8,128)(2,1)S(1)} %copy-done) | data formatting | bytes 4915200 | tf_op args[2]
  13.3 129.7 %shard_map.55 = bf16[32,160,128]{2,1,0:T(8,128)(2,1)} custom-call(s32[32]{0:T(128)} %select_reduce_fusion.source_ref, s32[16]{0:T(128)} %select_reduce_fusion.1.chosen_ref, s32[32]{0:T(128)} %get-tuple-element.6.back_ref, s32[32]{0:T(128)} %get-tuple-element.5.slot_ref, bf16[32,160,128]{2,1,0:T(8,128)(2,1)} %bitcast.17, ...), custom_call_target="tpu_custom_call" | custom-call | tf_op jit(solution)/shard_map/pallas_call | solution.py:371
  143.1 2.9 %copy.14 = bf16[4,8,160,128]{3,1,2,0:T(8,128)(2,1)} copy(bf16[4,8,160,128]{3,2,1,0:T(8,128)(2,1)} %bitcast.16) | data formatting | bytes 2621440
Async XLA Ops:
  7.0 2.8 %copy-start = (bf16[1280,960]{0,1:T(8,128)(2,1)S(1)}, bf16[1280,960]{0,1:T(8,128)(2,1)}, u32[]{:S(2)}) copy-start(bf16[1280,960]{0,1:T(8,128)(2,1)} %param.7) | copy-start | bytes 7372804

commit v2 on v1

--- a/solution.py
+++ b/solution.py
@@ -11,7 +11,7 @@
 WIN = 64
 ENC_WIN = 16
 LANES = 128
-PAIRS = 2
+PAIRS = 1
 
 epsilon = 1e-06
 MESH = pl.DeviceIdType.MESH
@@ -19,29 +19,105 @@
 BF16 = jnp.bfloat16
 
 
+SOURCE, CHOSEN, BACK, SLOT = range(4)
+
+
+def early_positions(n, cap):
+    return n - (ENC_WIN - 2 * PAIRS) // cap
+
+
+def position_order(n, cap):
+    far = list(range(n - 1, 1, -1))
+    split = early_positions(n, cap) - 3
+    return far[:split] + [1, 0] + far[split:]
+
+
+def position_of(flip, n, cap):
+    split = early_positions(n, cap) - 3
+    at = n - 1 - flip
+    at = jnp.where(at >= split, at + 2, at)
+    return jnp.where(flip == 1, split, jnp.where(flip == 0, split + 1, at))
+
+
+def partner(me, flip):
+    other, bit = me, 1
+    while bit <= flip:
+        if (flip // bit) % 2:
+            other = other + bit * (1 - 2 * ((me // bit) % 2))
+        bit *= 2
+    return other
+
+
+def iota(shape, axis):
+    return lax.broadcasted_iota(jnp.int32, shape, axis)
+
+
+def plan_indices(n, cap, me, plan_ref, index_v):
+    plan = plan_ref[...]
+    index_v[...] = jnp.zeros_like(index_v)
+    slots = plan.shape[1]
+    mine = plan_ref[pl.ds(me, 1), :]
+    same = iota((slots, slots), 0) == iota((slots, slots), 1)
+    turned = jnp.sum(jnp.where(same, mine, 0), axis=1, keepdims=True)
+    earlier = (turned == mine) & (iota((slots, slots), 1) < iota((slots, slots), 0))
+    ordinal = jnp.sum(earlier.astype(jnp.int32), axis=1, keepdims=True)
+    place = jnp.where(turned >= 0, position_of(turned ^ me, n, cap) * cap + ordinal, -1)
+    grid = (slots, n * cap)
+    source = jnp.sum(
+        jnp.where(place == iota(grid, 1), iota(grid, 0), 0), axis=0, keepdims=True
+    )
+    index_v[SOURCE:SOURCE + 1, :n * cap] = jnp.clip(source, 0, slots - 1)
+    index_v[SLOT:SLOT + 1, :slots] = jnp.minimum(
+        jnp.sum(jnp.where(same, place, 0), axis=0, keepdims=True), n * cap - 1
+    )
+
+    counts = jnp.sum((plan == me).astype(jnp.int32), axis=1, keepdims=True)
+    square = (n, n)
+    counts_row = jnp.sum(
+        jnp.where(iota(square, 0) == iota(square, 1), counts, 0), axis=0, keepdims=True
+    )
+    at_col = position_of(iota((n, 1), 0) ^ me, n, cap)
+    at_row = position_of(iota((1, n), 1) ^ me, n, cap)
+    offsets = jnp.sum(jnp.where(at_row < at_col, counts_row, 0), axis=1, keepdims=True)
+    j = iota((n, ENC_WIN), 1) - offsets
+    chosen = jnp.sum(
+        jnp.where((j >= 0) & (j < counts), at_col * cap + j, 0), axis=0, keepdims=True
+    )
+    index_v[CHOSEN:CHOSEN + 1, :ENC_WIN] = jnp.clip(chosen, 0, n * cap - 1)
+    q = iota((n, n * cap), 1)
+    back = jnp.sum(
+        jnp.where(q // cap == at_col, offsets + q % cap, 0), axis=0, keepdims=True
+    )
+    index_v[BACK:BACK + 1, :n * cap] = jnp.clip(back, 0, ENC_WIN - 1)
+
+
 def kernel(
     n, m, cap,
-    source_ref, chosen_ref, back_ref, slot_ref, x_ref, gain_ref, qkv_ref, outw_ref,
+    plan_ref, x_ref, gain_ref, qkv_ref, outw_ref,
     out_ref,
-    outb, inb, gath, qkv_t, outw_t, proj, heads, part, from_left, from_right, total, done, backb, homeb,
-    d_send, d_recv, b_send, b_recv, ag_recv, ag_right, ag_left, rs_send, rs_left, rs_right,
+    index_v, index_s, outw, gain_t, outb, inb, gath, qkv_t, outw_t, proj, heads, part, from_left, from_right, total, done, backb, homeb,
+    i_sem, w_sem, d_send, d_recv, b_send, b_recv, ag_recv, ag_right, ag_left, rs_send, rs_left, rs_right,
 ):
     me = lax.axis_index("dp")
     z = lax.axis_index("mp")
     home_win, rows, _ = x_ref.shape
     width = 2 * rows
     chunks = gath.shape[1]
-    heads_here = qkv_ref.shape[1] // (3 * HEAD_DIM)
+    heads_here = qkv_ref.shape[0] // (3 * HEAD_DIM)
+
+    order = position_order(n, cap)
+
+    load_qkv = pltpu.make_async_copy(qkv_ref, qkv_t, w_sem.at[0])
+    load_outw = pltpu.make_async_copy(outw_ref, outw, w_sem.at[1])
+    load_qkv.start()
+    load_outw.start()
 
     barrier = pltpu.get_barrier_semaphore()
 
-    def greet(d, _):
+    for d in range(1, n):
         pl.semaphore_signal(
-            barrier, inc=1, device_id={"dp": lax.rem(me + d, n)}, device_id_type=MESH
+            barrier, inc=1, device_id={"dp": partner(me, d)}, device_id_type=MESH
         )
-        return 0
-
-    lax.fori_loop(1, n, greet, 0)
 
     @pl.when(z > 0)
     def _():
@@ -51,47 +127,36 @@
     def _():
         pl.semaphore_signal(barrier, inc=1, device_id={"mp": z + 1}, device_id_type=MESH)
 
-    def pack(d, _):
-        e = lax.rem(me + d, n)
+    plan_indices(n, cap, me, plan_ref, index_v)
+    load_index = pltpu.make_async_copy(index_v, index_s, i_sem)
+    load_index.start()
+    load_index.wait()
+    for p in range(n):
         for j in range(cap):
-            outb[e, j] = x_ref[source_ref[e * cap + j]]
-        return 0
-
-    lax.fori_loop(0, n, pack, 0)
+            outb[p, j] = x_ref[index_s[SOURCE, p * cap + j]]
+
     ends = (z == 0).astype(jnp.int32) + (z == m - 1).astype(jnp.int32)
     pl.semaphore_wait(barrier, n + 1 - ends)
 
-    def exchange(src, dst, send, recv, d):
-        e = lax.rem(me + d, n)
+    own = order.index(0)
+
+    def exchange(src, dst, send, recv, p):
         return pltpu.make_async_remote_copy(
-            src_ref=src.at[e], dst_ref=dst.at[me], send_sem=send.at[d], recv_sem=recv.at[d],
-            device_id={"dp": e}, device_id_type=MESH,
+            src_ref=src.at[p], dst_ref=dst.at[p], send_sem=send.at[p], recv_sem=recv.at[p],
+            device_id={"dp": partner(me, order[p])}, device_id_type=MESH,
         )
 
-    def start_exchange(src, dst, send, recv):
-        def step(d, _):
-            exchange(src, dst, send, recv, d).start()
-            return 0
-
-        lax.fori_loop(1, n, step, 0)
-
-    def end_exchange(src, dst, send, recv):
-        def step(d, _):
-            exchange(src, dst, send, recv, d).wait()
-            return 0
-
-        lax.fori_loop(1, n, step, 0)
-
-    start_exchange(outb, inb, d_send, d_recv)
-    inb[me] = outb[me]
-
-    lower = 0
-    while lower < qkv_ref.shape[1]:
-        size = min(LANES, qkv_ref.shape[1] - lower)
-        qkv_t[lower:lower + size, :] = qkv_ref[:, lower:lower + size].T
-        lower += size
-    for lower in range(0, outw_ref.shape[1], LANES):
-        outw_t[lower:lower + LANES, :] = outw_ref[:, lower:lower + LANES].T
+    others = [p for p in range(n) if p != own]
+    for p in others:
+        exchange(outb, inb, d_send, d_recv, p).start()
+    inb[own] = outb[own]
+
+    load_outw.wait()
+    for lower in range(0, outw.shape[1], LANES):
+        outw_t[lower:lower + LANES, :] = outw[:, lower:lower + LANES].T
+        gain_t[lower:lower + LANES, :] = jnp.broadcast_to(
+            gain_ref[:, lower:lower + LANES], (LANES, LANES)
+        ).T
 
     row = lax.broadcasted_iota(jnp.int32, (width, width), 0)
     col = lax.broadcasted_iota(jnp.int32, (width, width), 1)
@@ -103,10 +168,12 @@
     ).astype(BF16)
     low_half = lax.broadcasted_iota(jnp.int32, (rows, LANES), 1) < WIN
 
-    end_exchange(outb, inb, d_send, d_recv)
+    for p in others:
+        exchange(outb, inb, d_send, d_recv, p).wait()
+    load_qkv.wait()
 
     def window_in(k):
-        at = chosen_ref[k]
+        at = index_s[CHOSEN, k]
         return inb[at // cap, lax.rem(at, cap)].astype(F32)
 
     def unpack(c, _):
@@ -209,7 +276,8 @@
     def project(c):
         full = gath[:, c].reshape(m * width, PAIRS * LANES).astype(F32)
         mean_square = jnp.mean(full * full, axis=0, keepdims=True)
-        normed = (full * lax.rsqrt(mean_square + epsilon) * gain_ref[...]).astype(BF16)
+        gain = jnp.concatenate([gain_t[...]] * PAIRS, axis=1)
+        normed = (full * lax.rsqrt(mean_square + epsilon) * gain).astype(BF16)
         proj[...] = jnp.dot(qkv_t[...], normed, preferred_element_type=F32).astype(BF16)
 
     key_window = lax.broadcasted_iota(jnp.int32, (LANES, LANES), 0) // WIN
@@ -246,7 +314,7 @@
     for t in range(1, m):
         ag_step(0, t)
 
-    between = PAIRS + 1
+    between = PAIRS + 2
 
     def steps_at(place):
         return [t for t in range(1, m) if (t - 1) * between // (m - 1) == place]
@@ -261,8 +329,10 @@
             def _():
                 if place == 0:
                     project(c)
+                elif place <= PAIRS:
+                    attend(place - 1)
                 else:
-                    attend(place - 1)
+                    output(c)
 
             @pl.when(c + 1 < chunks)
             def _():
@@ -279,22 +349,18 @@
 
         @pl.when(c < chunks)
         def _():
-            output(c)
             rs_stage(c, 0)
 
         return 0
 
     lax.fori_loop(0, chunks + 1, turn, 0)
 
-    def reply(d, _):
-        e = lax.rem(me + d, n)
+    for p in range(n):
         for j in range(cap):
-            backb[e, j] = done[back_ref[e * cap + j]]
-        return 0
-
-    lax.fori_loop(0, n, reply, 0)
-    start_exchange(backb, homeb, b_send, b_recv)
-    homeb[me] = backb[me]
+            backb[p, j] = done[index_s[BACK, p * cap + j]]
+        if p != own:
+            exchange(backb, homeb, b_send, b_recv, p).start()
+    homeb[own] = backb[own]
 
     def sent(c, _):
         def each(o, _):
@@ -319,10 +385,11 @@
         return lax.fori_loop(0, m, each, 0)
 
     lax.fori_loop(0, chunks, sent, 0)
-    end_exchange(backb, homeb, b_send, b_recv)
+    for p in others:
+        exchange(backb, homeb, b_send, b_recv, p).wait()
 
     def place_home(s, _):
-        at = slot_ref[s]
+        at = index_s[SLOT, s]
         safe = jnp.maximum(at, 0)
         found = homeb[safe // cap, lax.rem(safe, cap)].astype(F32)
         out_ref[s] = jnp.where(at >= 0, found, jnp.zeros_like(found)).astype(BF16)
@@ -334,7 +401,6 @@
 def body(patches, norm_gain, qkv_weight, out_weight, window_plan):
     n = lax.axis_size("dp")
     m = lax.axis_size("mp")
-    here = lax.axis_index("dp")
     home_win, row_width = patches.shape
     rows = row_width // LANES
     width = 2 * rows
@@ -343,37 +409,19 @@
     chunks = ENC_WIN // (2 * PAIRS)
     cols = PAIRS * LANES
 
-    my_plan = lax.dynamic_slice_in_dim(window_plan, here, 1, 0)[0]
-    slots = jnp.arange(home_win, dtype=jnp.int32)
-    earlier = (my_plan[:, None] == my_plan[None, :]) & (slots[None, :] < slots[:, None])
-    ordinal = jnp.sum(earlier.astype(jnp.int32), axis=1)
-    slot_index = jnp.where(my_plan >= 0, my_plan * cap + ordinal, -1)
-    all_slots = jnp.arange(n * cap, dtype=jnp.int32)
-    source = jnp.sum(
-        jnp.where(slot_index[None, :] == all_slots[:, None], slots[None, :], 0), axis=1
-    )
-    sent_here = jnp.sum((window_plan == here).astype(jnp.int32), axis=1)
-    homes = jnp.arange(n, dtype=jnp.int32)
-    offsets = jnp.sum(
-        jnp.where(homes[None, :] < homes[:, None], sent_here[None, :], 0), axis=1
-    )
-    columns = jnp.arange(cap, dtype=jnp.int32)
-    position = jnp.where(
-        columns[None, :] < sent_here[:, None], offsets[:, None] + columns[None, :], -1
-    ).reshape(n * cap)
-    picked = position[None, :] == jnp.arange(ENC_WIN, dtype=jnp.int32)[:, None]
-    chosen = jnp.sum(jnp.where(picked, all_slots[None, :], 0), axis=1)
-    back = jnp.maximum(position, 0)
-
-    smem = pl.BlockSpec(memory_space=pltpu.SMEM)
+    hbm = pl.BlockSpec(memory_space=pl.ANY)
     vmem = pl.BlockSpec(memory_space=pltpu.VMEM)
     dma = pltpu.SemaphoreType.DMA
     result = pl.pallas_call(
         functools.partial(kernel, n, m, cap),
         out_shape=jax.ShapeDtypeStruct((home_win, rows, LANES), BF16),
-        in_specs=[smem] * 4 + [vmem] * 4,
+        in_specs=[vmem] * 3 + [hbm] * 2,
         out_specs=vmem,
         scratch_shapes=[
+            pltpu.VMEM((8, LANES), jnp.int32),
+            pltpu.SMEM((8, LANES), jnp.int32),
+            pltpu.VMEM(out_weight.shape, BF16),
+            pltpu.VMEM((full_width, LANES), F32),
             pltpu.VMEM((n, cap, rows, LANES), BF16),
             pltpu.VMEM((n, cap, rows, LANES), BF16),
             pltpu.VMEM((m, chunks, width, cols), BF16),
@@ -388,7 +436,7 @@
             pltpu.VMEM((ENC_WIN, rows, LANES), BF16),
             pltpu.VMEM((n, cap, rows, LANES), BF16),
             pltpu.VMEM((n, cap, rows, LANES), BF16),
-            dma((n,)), dma((n,)), dma((n,)), dma((n,)),
+            dma, dma((2,)), dma((n,)), dma((n,)), dma((n,)), dma((n,)),
             dma((chunks, m)), dma((chunks, m)), dma((chunks, m)),
             dma((chunks, m)), dma((chunks, m)), dma((chunks, m)),
         ],
@@ -396,8 +444,8 @@
             collective_id=0, has_side_effects=True, vmem_limit_bytes=56 * 1024 * 1024
         ),
     )(
-        source, chosen, back, slot_index,
-        patches.reshape(home_win, rows, LANES), norm_gain[:, None], qkv_weight, out_weight,
+        window_plan, patches.reshape(home_win, rows, LANES), norm_gain[None, :],
+        qkv_weight.T, out_weight,
     )
     return result.reshape(home_win, row_width)
 

time: 148 us -> 153 us (1.034)
  Pallas kernels: 130 us -> 144 us
  local copies, waits for them, and re-layouts: 11.8 us -> 6.78 us
  other arithmetic: 4.44 us -> 0 us
    pallas_call x1, Pallas kernels: 130 us -> 144 us  [body(): pl.pallas_call(functools.partial(kernel, n, m, cap), out_shape=jax.ShapeD...]
    unnamed x5 -> x2, local copies, waits for them, and re-layouts: 9.23 us -> 5.49 us
    reduce_sum x5 -> x0, other arithmetic: 2.41 us -> none  [the longest x1 0.8 us: body(): sent_here = jnp.sum((window_plan == here).astype(jnp.int32), axis=1)]
where the time goes in v2:
time: 153 us; the launch traced here: 151 us
  Pallas kernels  144 us (94%)
  local copies, waits for them, and re-layouts  6.78 us (4%)
    pallas_call x1, Pallas kernels, body(): pl.pallas_call(functools.partial(kernel, n, m, cap), out_shape=jax.ShapeD...  144 us
    unnamed x2, local copies, waits for them, and re-layouts  5.49 us

profile of v2, /device:TPU:1, one launch (start us, length us, event | category | flops | bytes accessed | tf_op | source)
XLA Modules:
  0.0 150.9 jit_solution(15941845211319062739)
XLA Ops:
  0.0 1.3 broadcast_in_dim.3.gain_ref
  1.3 2.6 %copy.6 = bf16[4,8,160,128]{3,2,1,0:T(8,128)(2,1)} copy(bf16[4,8,160,128]{3,1,2,0:T(8,128)(2,1)} %bitcast.10) | data formatting | bytes 2621440
  3.9 144.1 %shard_map.55 = bf16[32,160,128]{2,1,0:T(8,128)(2,1)} custom-call(s32[8,32]{1,0:T(8,128)} %plan_ref.1, bf16[32,160,128]{2,1,0:T(8,128)(2,1)} %bitcast.8, f32[1,1280]{1,0:T(1,128)} %broadcast_in_dim.3.gain_ref, bf16[960,1280]{1,0:T(8,128)(2,1)} %bitcast.9, bf16[320,1280]{1,0:T(8,128)(2,1)} %outw_ref.1), custom_call_target="tpu_custom_call" | custom-call | tf_op jit(solution)/shard_map/pallas_call | solution.py:415
  148.1 2.9 %copy.9 = bf16[4,8,160,128]{3,1,2,0:T(8,128)(2,1)} copy(bf16[4,8,160,128]{3,2,1,0:T(8,128)(2,1)} %bitcast.7) | data formatting | bytes 2621440

commit v3 on v2

--- a/solution.py
+++ b/solution.py
@@ -13,6 +13,7 @@
 LANES = 128
 PAIRS = 1
 
+LOG2E = 1.4426950408889634
 epsilon = 1e-06
 MESH = pl.DeviceIdType.MESH
 F32 = jnp.float32
@@ -293,10 +294,11 @@
             value_vecs = proj[base + 2 * HEAD_DIM:base + 3 * HEAD_DIM, lanes]
             scores = lax.dot_general(
                 key_vecs, queries, (((0,), (0,)), ((), ())), preferred_element_type=F32
-            ) * HEAD_DIM ** (-0.5)
+            ) * (HEAD_DIM ** (-0.5) * LOG2E)
             scores = jnp.where(same_window, scores, -1e30)
-            weights = jnp.exp(scores - jnp.max(scores, axis=0, keepdims=True))
-            probs = (weights / jnp.sum(weights, axis=0, keepdims=True)).astype(BF16)
+            weights = jnp.exp2(scores - jnp.max(scores, axis=0, keepdims=True))
+            scale = 1.0 / jnp.sum(weights, axis=0, keepdims=True)
+            probs = (weights * scale).astype(BF16)
             heads[h * HEAD_DIM:(h + 1) * HEAD_DIM, lanes] = jnp.dot(
                 value_vecs, probs, preferred_element_type=F32
             ).astype(BF16)
@@ -308,52 +310,31 @@
             ).astype(BF16)
 
     lax.fori_loop(0, chunks, unpack, 0)
-    ag_own(0)
-    if chunks > 1:
-        ag_own(1)
-    for t in range(1, m):
-        ag_step(0, t)
-
-    between = PAIRS + 2
-
-    def steps_at(place):
-        return [t for t in range(1, m) if (t - 1) * between // (m - 1) == place]
-
-    def turn(c, _):
-        @pl.when(c + 2 < chunks)
-        def _():
-            ag_own(c + 2)
-
-        for place in range(between):
-            @pl.when(c < chunks)
-            def _():
-                if place == 0:
-                    project(c)
-                elif place <= PAIRS:
-                    attend(place - 1)
-                else:
-                    output(c)
-
-            @pl.when(c + 1 < chunks)
-            def _():
-                for t in steps_at(place):
-                    ag_step(c + 1, t)
-
-            @pl.when(c > 0)
-            def _():
-                for t in steps_at(place):
-                    if t < m - 1:
-                        rs_stage(c - 1, t)
-                    else:
-                        rs_final(c - 1)
-
-        @pl.when(c < chunks)
-        def _():
-            rs_stage(c, 0)
-
+
+    def within(c, act):
+        @pl.when(jnp.logical_and(c >= 0, c < chunks))
+        def _():
+            act(c)
+
+    def compute(c):
+        project(c)
+        for p in range(PAIRS):
+            attend(p)
+        output(c)
+
+    def turn(i, _):
+        c = i - (m - 1)
+        for t in range(m - 1, 0, -1):
+            within(c + m - 1 - t, lambda at, t=t: ag_step(at, t))
+        within(c + m - 1, ag_own)
+        within(c, compute)
+        within(c, lambda at: rs_stage(at, 0))
+        for k in range(1, m - 1):
+            within(c - k, lambda at, k=k: rs_stage(at, k))
+        within(c - (m - 1), rs_final)
         return 0
 
-    lax.fori_loop(0, chunks + 1, turn, 0)
+    lax.fori_loop(0, chunks + 2 * (m - 1), turn, 0)
 
     for p in range(n):
         for j in range(cap):

time: 153 us -> 119 us (0.78)
  Pallas kernels: 144 us -> 110 us
    pallas_call x1, Pallas kernels: 144 us -> 110 us  [body(): pl.pallas_call(functools.partial(kernel, n, m, cap), out_shape=jax.ShapeD...]
where the time goes in v3:
time: 119 us; the launch traced here: 116 us
  Pallas kernels  110 us (92%)
  local copies, waits for them, and re-layouts  6.78 us (6%)
    pallas_call x1, Pallas kernels, body(): pl.pallas_call(functools.partial(kernel, n, m, cap), out_shape=jax.ShapeD...  110 us
    unnamed x2, local copies, waits for them, and re-layouts  5.49 us

profile of v3, /device:TPU:1, one launch (start us, length us, event | category | flops | bytes accessed | tf_op | source)
XLA Modules:
  0.0 116.5 jit_solution(12007236134090867199)
XLA Ops:
  0.0 1.3 %broadcast_in_dim.3.gain_ref = f32[1,1280]{1,0:T(1,128)} reshape(f32[1280]{0:T(1024)} %param.6) | data formatting | bytes 10240 | tf_op jit(solution)/shard_map/broadcast_in_dim | solution.py:428
  1.3 2.6 %copy.6 = bf16[4,8,160,128]{3,2,1,0:T(8,128)(2,1)} copy(bf16[4,8,160,128]{3,1,2,0:T(8,128)(2,1)} %bitcast.10) | data formatting | bytes 2621440
  3.9 109.7 %shard_map.55 = bf16[32,160,128]{2,1,0:T(8,128)(2,1)} custom-call(s32[8,32]{1,0:T(8,128)} %plan_ref.1, bf16[32,160,128]{2,1,0:T(8,128)(2,1)} %bitcast.8, f32[1,1280]{1,0:T(1,128)} %broadcast_in_dim.3.gain_ref, bf16[960,1280]{1,0:T(8,128)(2,1)} %bitcast.9, bf16[320,1280]{1,0:T(8,128)(2,1)} %outw_ref.1), custom_call_target="tpu_custom_call" | custom-call | tf_op jit(solution)/shard_map/pallas_call | solution.py:396
  113.6 2.9 %copy.9 = bf16[4,8,160,128]{3,1,2,0:T(8,128)(2,1)} copy(bf16[4,8,160,128]{3,2,1,0:T(8,128)(2,1)} %bitcast.7) | data formatting | bytes 2621440

commit v4 on v3

--- a/solution.py
+++ b/solution.py
@@ -29,12 +29,12 @@
 
 def position_order(n, cap):
     far = list(range(n - 1, 1, -1))
-    split = early_positions(n, cap) - 3
+    split = early_positions(n, cap) - 2
     return far[:split] + [1, 0] + far[split:]
 
 
 def position_of(flip, n, cap):
-    split = early_positions(n, cap) - 3
+    split = early_positions(n, cap) - 2
     at = n - 1 - flip
     at = jnp.where(at >= split, at + 2, at)
     return jnp.where(flip == 1, split, jnp.where(flip == 0, split + 1, at))
@@ -96,7 +96,7 @@
     n, m, cap,
     plan_ref, x_ref, gain_ref, qkv_ref, outw_ref,
     out_ref,
-    index_v, index_s, outw, gain_t, outb, inb, gath, qkv_t, outw_t, proj, heads, part, from_left, from_right, total, done, backb, homeb,
+    index_v, index_s, outw, gain_t, outb, inb, inb_late, gath, qkv_t, outw_t, proj, heads, part, from_left, from_right, total, done, backb, homeb,
     i_sem, w_sem, d_send, d_recv, b_send, b_recv, ag_recv, ag_right, ag_left, rs_send, rs_left, rs_right,
 ):
     me = lax.axis_index("dp")
@@ -141,15 +141,27 @@
 
     own = order.index(0)
 
-    def exchange(src, dst, send, recv, p):
+    own = order.index(0)
+    early = early_positions(n, cap)
+
+    def exchange(src, dst, send, recv, p, at):
         return pltpu.make_async_remote_copy(
-            src_ref=src.at[p], dst_ref=dst.at[p], send_sem=send.at[p], recv_sem=recv.at[p],
+            src_ref=src.at[p], dst_ref=dst.at[at], send_sem=send.at[p], recv_sem=recv.at[p],
             device_id={"dp": partner(me, order[p])}, device_id_type=MESH,
         )
 
+    def dispatch(p):
+        if p < early:
+            return exchange(outb, inb, d_send, d_recv, p, p)
+        return exchange(outb, inb_late, d_send, d_recv, p, p - early)
+
+    def reply(p):
+        return exchange(backb, homeb, b_send, b_recv, p, p)
+
     others = [p for p in range(n) if p != own]
     for p in others:
-        exchange(outb, inb, d_send, d_recv, p).start()
+        if p < early:
+            dispatch(p).start()
     inb[own] = outb[own]
 
     load_outw.wait()
@@ -170,14 +182,24 @@
     low_half = lax.broadcasted_iota(jnp.int32, (rows, LANES), 1) < WIN
 
     for p in others:
-        exchange(outb, inb, d_send, d_recv, p).wait()
+        if p >= early:
+            dispatch(p).start()
     load_qkv.wait()
-
-    def window_in(k):
+    for p in others:
+        if p < early:
+            dispatch(p).wait()
+
+    def window_early(k):
+        at = jnp.minimum(index_s[CHOSEN, k], early * cap - 1)
+        return inb[at // cap, lax.rem(at, cap)].astype(F32)
+
+    def window_any(k):
         at = index_s[CHOSEN, k]
-        return inb[at // cap, lax.rem(at, cap)].astype(F32)
-
-    def unpack(c, _):
+        late = jnp.maximum(at - early * cap, 0)
+        found = inb_late[late // cap, lax.rem(late, cap)].astype(F32)
+        return jnp.where(at < early * cap, window_early(k), found)
+
+    def unpack(c, window_in):
         for p in range(PAIRS):
             first = window_in((c * PAIRS + p) * 2)
             second = window_in((c * PAIRS + p) * 2 + 1)
@@ -186,7 +208,6 @@
             halves = jnp.concatenate([even, odd], axis=0).astype(BF16)
             block = jnp.dot(spread, halves, preferred_element_type=F32).astype(BF16)
             gath[z, c, :, p * LANES:(p + 1) * LANES] = block
-        return 0
 
     def ag_copy(c, o, step, send):
         return pltpu.make_async_remote_copy(
@@ -309,7 +330,44 @@
                 outw_t[s * width:(s + 1) * width, :], heads[...], preferred_element_type=F32
             ).astype(BF16)
 
-    lax.fori_loop(0, chunks, unpack, 0)
+    chunk_win = 2 * PAIRS
+    early_chunks = sum(
+        n - (ENC_WIN - (c + 1) * chunk_win) // cap <= early for c in range(chunks)
+    )
+
+    def own_chunk(c):
+        @pl.when(c < early_chunks)
+        def _():
+            unpack(c, window_early)
+
+        if early_chunks < chunks:
+            @pl.when(c == early_chunks)
+            def _():
+                for p in others:
+                    if p >= early:
+                        dispatch(p).wait()
+
+            @pl.when(c >= early_chunks)
+            def _():
+                unpack(c, window_any)
+
+        ag_own(c)
+
+    def ready(p):
+        return (min(ENC_WIN, cap * (p + 1)) - 1) // chunk_win
+
+    def answer(p):
+        for j in range(cap):
+            backb[p, j] = done[index_s[BACK, p * cap + j]]
+        if p != own:
+            reply(p).start()
+
+    def finish(c):
+        rs_final(c)
+        for p in range(n):
+            if ready(p) < chunks - 1:
+                pl.when(c == ready(p))(functools.partial(answer, p))
+
 
     def within(c, act):
         @pl.when(jnp.logical_and(c >= 0, c < chunks))
@@ -326,21 +384,19 @@
         c = i - (m - 1)
         for t in range(m - 1, 0, -1):
             within(c + m - 1 - t, lambda at, t=t: ag_step(at, t))
-        within(c + m - 1, ag_own)
+        within(c + m - 1, own_chunk)
         within(c, compute)
         within(c, lambda at: rs_stage(at, 0))
         for k in range(1, m - 1):
             within(c - k, lambda at, k=k: rs_stage(at, k))
-        within(c - (m - 1), rs_final)
+        within(c - (m - 1), finish)
         return 0
 
     lax.fori_loop(0, chunks + 2 * (m - 1), turn, 0)
 
     for p in range(n):
-        for j in range(cap):
-            backb[p, j] = done[index_s[BACK, p * cap + j]]
-        if p != own:
-            exchange(backb, homeb, b_send, b_recv, p).start()
+        if ready(p) == chunks - 1:
+            answer(p)
     homeb[own] = backb[own]
 
     def sent(c, _):
@@ -367,7 +423,7 @@
 
     lax.fori_loop(0, chunks, sent, 0)
     for p in others:
-        exchange(backb, homeb, b_send, b_recv, p).wait()
+        reply(p).wait()
 
     def place_home(s, _):
         at = index_s[SLOT, s]
@@ -389,6 +445,7 @@
     cap = (home_win + n - 1) // n
     chunks = ENC_WIN // (2 * PAIRS)
     cols = PAIRS * LANES
+    early = early_positions(n, cap)
 
     hbm = pl.BlockSpec(memory_space=pl.ANY)
     vmem = pl.BlockSpec(memory_space=pltpu.VMEM)
@@ -404,7 +461,8 @@
             pltpu.VMEM(out_weight.shape, BF16),
             pltpu.VMEM((full_width, LANES), F32),
             pltpu.VMEM((n, cap, rows, LANES), BF16),
-            pltpu.VMEM((n, cap, rows, LANES), BF16),
+            pltpu.VMEM((early, cap, rows, LANES), BF16),
+            pltpu.VMEM((n - early, cap, rows, LANES), BF16),
             pltpu.VMEM((m, chunks, width, cols), BF16),
             pltpu.VMEM((qkv_weight.shape[1], full_width), BF16),
             pltpu.VMEM((full_width, out_weight.shape[0]), BF16),

time: 119 us -> 109 us (0.916)
  the two profiles are of different devices: /device:TPU:1 before, /device:TPU:0 now
where the time goes in v4:
time: 109 us
  Pallas kernels  102 us (94%)
  local copies, waits for them, and re-layouts  6.78 us (6%)
    pallas_call x1, Pallas kernels, body(): pl.pallas_call(functools.partial(kernel, n, m, cap), out_shape=jax.ShapeD...  102 us
    unnamed x2, local copies, waits for them, and re-layouts  5.49 us

profile of v4, /device:TPU:0, one launch (start us, length us, event | category | flops | bytes accessed | tf_op | source)
XLA Modules:
  0.0 108.6 jit_solution(2220528381624552996)
XLA Ops:
  0.0 1.3 %broadcast_in_dim.3.gain_ref = f32[1,1280]{1,0:T(1,128)} reshape(f32[1280]{0:T(1024)} %param.6) | data formatting | bytes 10240 | tf_op jit(solution)/shard_map/broadcast_in_dim | solution.py:486
  1.3 2.6 %copy.6 = bf16[4,8,160,128]{3,2,1,0:T(8,128)(2,1)} copy(bf16[4,8,160,128]{3,1,2,0:T(8,128)(2,1)} %bitcast.10) | data formatting | bytes 2621440
  3.9 101.8 %shard_map.55 = bf16[32,160,128]{2,1,0:T(8,128)(2,1)} custom-call(s32[8,32]{1,0:T(8,128)} %plan_ref.1, bf16[32,160,128]{2,1,0:T(8,128)(2,1)} %bitcast.8, f32[1,1280]{1,0:T(1,128)} %broadcast_in_dim.3.gain_ref, bf16[960,1280]{1,0:T(8,128)(2,1)} %bitcast.9, bf16[320,1280]{1,0:T(8,128)(2,1)} %outw_ref.1), custom_call_target="tpu_custom_call" | custom-call | tf_op jit(solution)/shard_map/pallas_call | solution.py:453
  105.7 2.9 %copy.9 = bf16[4,8,160,128]{3,1,2,0:T(8,128)(2,1)} copy(bf16[4,8,160,128]{3,2,1,0:T(8,128)(2,1)} %bitcast.7) | data formatting | bytes 2621440

commit v5 on v4

--- a/solution.py
+++ b/solution.py
@@ -28,14 +28,14 @@
 
 
 def position_order(n, cap):
-    far = list(range(n - 1, 1, -1))
+    far = list(range(n - 2, 1, -2)) + list(range(n - 1, 2, -2))
     split = early_positions(n, cap) - 2
     return far[:split] + [1, 0] + far[split:]
 
 
 def position_of(flip, n, cap):
     split = early_positions(n, cap) - 2
-    at = n - 1 - flip
+    at = jnp.where(flip % 2 == 0, (n - 2 - flip) // 2, n // 2 - 1 + (n - 1 - flip) // 2)
     at = jnp.where(at >= split, at + 2, at)
     return jnp.where(flip == 1, split, jnp.where(flip == 0, split + 1, at))
 
@@ -62,14 +62,14 @@
     turned = jnp.sum(jnp.where(same, mine, 0), axis=1, keepdims=True)
     earlier = (turned == mine) & (iota((slots, slots), 1) < iota((slots, slots), 0))
     ordinal = jnp.sum(earlier.astype(jnp.int32), axis=1, keepdims=True)
-    place = jnp.where(turned >= 0, position_of(turned ^ me, n, cap) * cap + ordinal, -1)
+    place = jnp.where(turned >= 0, position_of(turned ^ me, n, cap) * cap + ordinal, n * cap)
     grid = (slots, n * cap)
     source = jnp.sum(
         jnp.where(place == iota(grid, 1), iota(grid, 0), 0), axis=0, keepdims=True
     )
     index_v[SOURCE:SOURCE + 1, :n * cap] = jnp.clip(source, 0, slots - 1)
     index_v[SLOT:SLOT + 1, :slots] = jnp.minimum(
-        jnp.sum(jnp.where(same, place, 0), axis=0, keepdims=True), n * cap - 1
+        jnp.sum(jnp.where(same, place, 0), axis=0, keepdims=True), n * cap
     )
 
     counts = jnp.sum((plan == me).astype(jnp.int32), axis=1, keepdims=True)
@@ -168,7 +168,7 @@
     for lower in range(0, outw.shape[1], LANES):
         outw_t[lower:lower + LANES, :] = outw[:, lower:lower + LANES].T
         gain_t[lower:lower + LANES, :] = jnp.broadcast_to(
-            gain_ref[:, lower:lower + LANES], (LANES, LANES)
+            gain_ref[lower // LANES:lower // LANES + 1, :], (LANES, LANES)
         ).T
 
     row = lax.broadcasted_iota(jnp.int32, (width, width), 0)
@@ -302,9 +302,7 @@
         normed = (full * lax.rsqrt(mean_square + epsilon) * gain).astype(BF16)
         proj[...] = jnp.dot(qkv_t[...], normed, preferred_element_type=F32).astype(BF16)
 
-    key_window = lax.broadcasted_iota(jnp.int32, (LANES, LANES), 0) // WIN
-    query_window = lax.broadcasted_iota(jnp.int32, (LANES, LANES), 1) // WIN
-    same_window = key_window == query_window
+    first_window = iota((WIN, LANES), 1) < WIN
 
     def attend(p):
         lanes = slice(p * LANES, (p + 1) * LANES)
@@ -316,10 +314,13 @@
             scores = lax.dot_general(
                 key_vecs, queries, (((0,), (0,)), ((), ())), preferred_element_type=F32
             ) * (HEAD_DIM ** (-0.5) * LOG2E)
-            scores = jnp.where(same_window, scores, -1e30)
+            scores = jnp.where(first_window, scores[:WIN], scores[WIN:])
             weights = jnp.exp2(scores - jnp.max(scores, axis=0, keepdims=True))
             scale = 1.0 / jnp.sum(weights, axis=0, keepdims=True)
-            probs = (weights * scale).astype(BF16)
+            probs = weights * scale
+            probs = jnp.concatenate(
+                [jnp.where(first_window, probs, 0.0), jnp.where(first_window, 0.0, probs)], axis=0
+            ).astype(BF16)
             heads[h * HEAD_DIM:(h + 1) * HEAD_DIM, lanes] = jnp.dot(
                 value_vecs, probs, preferred_element_type=F32
             ).astype(BF16)
@@ -398,6 +399,7 @@
         if ready(p) == chunks - 1:
             answer(p)
     homeb[own] = backb[own]
+    homeb[n] = jnp.zeros_like(homeb[n])
 
     def sent(c, _):
         def each(o, _):
@@ -427,9 +429,7 @@
 
     def place_home(s, _):
         at = index_s[SLOT, s]
-        safe = jnp.maximum(at, 0)
-        found = homeb[safe // cap, lax.rem(safe, cap)].astype(F32)
-        out_ref[s] = jnp.where(at >= 0, found, jnp.zeros_like(found)).astype(BF16)
+        out_ref[s] = homeb[at // cap, lax.rem(at, cap)]
         return 0
 
     lax.fori_loop(0, home_win, place_home, 0)
@@ -474,7 +474,7 @@
             pltpu.VMEM((width, cols), F32),
             pltpu.VMEM((ENC_WIN, rows, LANES), BF16),
             pltpu.VMEM((n, cap, rows, LANES), BF16),
-            pltpu.VMEM((n, cap, rows, LANES), BF16),
+            pltpu.VMEM((n + 1, cap, rows, LANES), BF16),
             dma, dma((2,)), dma((n,)), dma((n,)), dma((n,)), dma((n,)),
             dma((chunks, m)), dma((chunks, m)), dma((chunks, m)),
             dma((chunks, m)), dma((chunks, m)), dma((chunks, m)),
@@ -483,7 +483,7 @@
             collective_id=0, has_side_effects=True, vmem_limit_bytes=56 * 1024 * 1024
         ),
     )(
-        window_plan, patches.reshape(home_win, rows, LANES), norm_gain[None, :],
+        window_plan, patches.reshape(home_win, rows, LANES), norm_gain.reshape(-1, LANES),
         qkv_weight.T, out_weight,
     )
     return result.reshape(home_win, row_width)

time: 109 us -> 103 us (0.945)
  the two profiles are of different devices: /device:TPU:0 before, /device:TPU:1 now
where the time goes in v5:
time: 103 us
  Pallas kernels  97.1 us (94%)
  local copies, waits for them, and re-layouts  5.49 us (5%)
    pallas_call x1, Pallas kernels, body(): pl.pallas_call(functools.partial(kernel, n, m, cap), out_shape=jax.ShapeD...  97.1 us
    unnamed x2, local copies, waits for them, and re-layouts  5.49 us

profile of v5, /device:TPU:1, one launch (start us, length us, event | category | flops | bytes accessed | tf_op | source)
XLA Modules:
  0.0 102.6 jit_solution(9353242276174732923)
XLA Ops:
  0.0 2.6 %copy.6 = bf16[4,8,160,128]{3,2,1,0:T(8,128)(2,1)} copy(bf16[4,8,160,128]{3,1,2,0:T(8,128)(2,1)} %bitcast.11) | data formatting | bytes 2621440
  2.6 97.1 %shard_map.55 = bf16[32,160,128]{2,1,0:T(8,128)(2,1)} custom-call(s32[8,32]{1,0:T(8,128)} %plan_ref.1, bf16[32,160,128]{2,1,0:T(8,128)(2,1)} %bitcast.9, f32[10,128]{1,0:T(8,128)} %bitcast.12, bf16[960,1280]{1,0:T(8,128)(2,1)} %bitcast.10, bf16[320,1280]{1,0:T(8,128)(2,1)} %outw_ref.1), custom_call_target="tpu_custom_call" | custom-call | tf_op jit(solution)/shard_map/pallas_call | solution.py:453
  99.7 2.9 %copy.9 = bf16[4,8,160,128]{3,1,2,0:T(8,128)(2,1)} copy(bf16[4,8,160,128]{3,2,1,0:T(8,128)(2,1)} %bitcast.8) | data formatting | bytes 2621440

commit v6 on v5

--- a/solution.py
+++ b/solution.py
@@ -25,6 +25,27 @@
 
 def early_positions(n, cap):
     return n - (ENC_WIN - 2 * PAIRS) // cap
+
+
+def arrival_stages(n, cap):
+    early, reach = early_positions(n, cap), min(cap, 2 * PAIRS)
+    stages = [(0, early, 0, reach), (0, early, reach, cap)]
+    stages += [(early, early + 1, 0, cap), (early + 1, n, 0, cap)]
+    return [part for part in stages if part[0] < part[1] and part[2] < part[3]]
+
+
+def early_stages(n, cap):
+    return sum(part[0] == 0 for part in arrival_stages(n, cap))
+
+
+def stages_needed(n, cap, c):
+    last = (c + 1) * 2 * PAIRS - 1
+    positions = n - (ENC_WIN - 1 - last) // cap
+    return max(
+        at + 1
+        for at, (low, _, first, _) in enumerate(arrival_stages(n, cap))
+        if low < positions and first <= last
+    )
 
 
 def position_order(n, cap):
@@ -96,7 +117,7 @@
     n, m, cap,
     plan_ref, x_ref, gain_ref, qkv_ref, outw_ref,
     out_ref,
-    index_v, index_s, outw, gain_t, outb, inb, inb_late, gath, qkv_t, outw_t, proj, heads, part, from_left, from_right, total, done, backb, homeb,
+    index_v, index_s, outw, gain_t, outb, inbs, gath, qkv_t, outw_t, proj, heads, part, from_left, from_right, total, done, backb, homeb,
     i_sem, w_sem, d_send, d_recv, b_send, b_recv, ag_recv, ag_right, ag_left, rs_send, rs_left, rs_right,
 ):
     me = lax.axis_index("dp")
@@ -142,7 +163,8 @@
     own = order.index(0)
 
     own = order.index(0)
-    early = early_positions(n, cap)
+    stages = arrival_stages(n, cap)
+    begun = early_stages(n, cap)
 
     def exchange(src, dst, send, recv, p, at):
         return pltpu.make_async_remote_copy(
@@ -150,19 +172,27 @@
             device_id={"dp": partner(me, order[p])}, device_id_type=MESH,
         )
 
-    def dispatch(p):
-        if p < early:
-            return exchange(outb, inb, d_send, d_recv, p, p)
-        return exchange(outb, inb_late, d_send, d_recv, p, p - early)
+    def dispatch(stage, p):
+        low, _, first, end = stages[stage]
+        return pltpu.make_async_remote_copy(
+            src_ref=outb.at[p, pl.ds(first, end - first)], dst_ref=inbs[stage].at[p - low],
+            send_sem=d_send.at[stage, p], recv_sem=d_recv.at[stage, p],
+            device_id={"dp": partner(me, order[p])}, device_id_type=MESH,
+        )
+
+    def senders(stage):
+        return [p for p in range(stages[stage][0], stages[stage][1]) if p != own]
 
     def reply(p):
         return exchange(backb, homeb, b_send, b_recv, p, p)
 
     others = [p for p in range(n) if p != own]
-    for p in others:
-        if p < early:
-            dispatch(p).start()
-    inb[own] = outb[own]
+    for stage in range(begun):
+        for p in senders(stage):
+            dispatch(stage, p).start()
+    for stage, (low, high, first, end) in enumerate(stages):
+        if low <= own < high:
+            inbs[stage][own - low] = outb[own, first:end]
 
     load_outw.wait()
     for lower in range(0, outw.shape[1], LANES):
@@ -181,28 +211,32 @@
     ).astype(BF16)
     low_half = lax.broadcasted_iota(jnp.int32, (rows, LANES), 1) < WIN
 
-    for p in others:
-        if p >= early:
-            dispatch(p).start()
+    for stage in range(begun, len(stages)):
+        for p in senders(stage):
+            dispatch(stage, p).start()
     load_qkv.wait()
-    for p in others:
-        if p < early:
-            dispatch(p).wait()
-
-    def window_early(k):
-        at = jnp.minimum(index_s[CHOSEN, k], early * cap - 1)
-        return inb[at // cap, lax.rem(at, cap)].astype(F32)
-
-    def window_any(k):
+    for p in senders(0):
+        dispatch(0, p).wait()
+
+    def window_in(k, upto):
         at = index_s[CHOSEN, k]
-        late = jnp.maximum(at - early * cap, 0)
-        found = inb_late[late // cap, lax.rem(late, cap)].astype(F32)
-        return jnp.where(at < early * cap, window_early(k), found)
-
-    def unpack(c, window_in):
+        p, j = at // cap, lax.rem(at, cap)
+        found = None
+        for (low, high, first, end), landed in zip(stages[:upto], inbs[:upto]):
+            part_p = jnp.clip(p, low, high - 1) - low
+            part_j = jnp.clip(j, first, end - 1) - first
+            value = landed[part_p, part_j].astype(F32)
+            if found is None:
+                found = value
+            else:
+                here = (p >= low) & (p < high) & (j >= first) & (j < end)
+                found = jnp.where(here, value, found)
+        return found
+
+    def unpack(c, upto):
         for p in range(PAIRS):
-            first = window_in((c * PAIRS + p) * 2)
-            second = window_in((c * PAIRS + p) * 2 + 1)
+            first = window_in((c * PAIRS + p) * 2, upto)
+            second = window_in((c * PAIRS + p) * 2 + 1, upto)
             even = jnp.where(low_half, first, pltpu.roll(second, WIN, 1))
             odd = jnp.where(low_half, pltpu.roll(first, WIN, 1), second)
             halves = jnp.concatenate([even, odd], axis=0).astype(BF16)
@@ -306,23 +340,27 @@
 
     def attend(p):
         lanes = slice(p * LANES, (p + 1) * LANES)
+        scores = []
         for h in range(heads_here):
             base = h * 3 * HEAD_DIM
             queries = proj[base:base + HEAD_DIM, lanes]
             key_vecs = proj[base + HEAD_DIM:base + 2 * HEAD_DIM, lanes]
+            both = lax.dot_general(
+                key_vecs, queries, (((0,), (0,)), ((), ())), preferred_element_type=F32
+            )
+            scores.append(jnp.where(first_window, both[:WIN], both[WIN:]))
+        scores = jnp.concatenate(scores, axis=1) * (HEAD_DIM ** (-0.5) * LOG2E)
+        weights = jnp.exp2(scores - jnp.max(scores, axis=0, keepdims=True))
+        probs = weights * (1.0 / jnp.sum(weights, axis=0, keepdims=True))
+        for h in range(heads_here):
+            base = h * 3 * HEAD_DIM
             value_vecs = proj[base + 2 * HEAD_DIM:base + 3 * HEAD_DIM, lanes]
-            scores = lax.dot_general(
-                key_vecs, queries, (((0,), (0,)), ((), ())), preferred_element_type=F32
-            ) * (HEAD_DIM ** (-0.5) * LOG2E)
-            scores = jnp.where(first_window, scores[:WIN], scores[WIN:])
-            weights = jnp.exp2(scores - jnp.max(scores, axis=0, keepdims=True))
-            scale = 1.0 / jnp.sum(weights, axis=0, keepdims=True)
-            probs = weights * scale
-            probs = jnp.concatenate(
-                [jnp.where(first_window, probs, 0.0), jnp.where(first_window, 0.0, probs)], axis=0
+            mine = probs[:, h * LANES:(h + 1) * LANES]
+            spread_probs = jnp.concatenate(
+                [jnp.where(first_window, mine, 0.0), jnp.where(first_window, 0.0, mine)], axis=0
             ).astype(BF16)
             heads[h * HEAD_DIM:(h + 1) * HEAD_DIM, lanes] = jnp.dot(
-                value_vecs, probs, preferred_element_type=F32
+                value_vecs, spread_probs, preferred_element_type=F32
             ).astype(BF16)
 
     def output(c):
@@ -332,25 +370,21 @@
             ).astype(BF16)
 
     chunk_win = 2 * PAIRS
-    early_chunks = sum(
-        n - (ENC_WIN - (c + 1) * chunk_win) // cap <= early for c in range(chunks)
-    )
+    needed = [stages_needed(n, cap, c) for c in range(chunks)]
 
     def own_chunk(c):
-        @pl.when(c < early_chunks)
-        def _():
-            unpack(c, window_early)
-
-        if early_chunks < chunks:
-            @pl.when(c == early_chunks)
-            def _():
-                for p in others:
-                    if p >= early:
-                        dispatch(p).wait()
-
-            @pl.when(c >= early_chunks)
-            def _():
-                unpack(c, window_any)
+        for stage in range(1, len(stages)):
+            @pl.when(c == sum(upto <= stage for upto in needed))
+            def _():
+                for p in senders(stage):
+                    dispatch(stage, p).wait()
+
+        for upto in sorted(set(needed)):
+            low = needed.index(upto)
+
+            @pl.when(jnp.logical_and(c >= low, c < low + needed.count(upto)))
+            def _():
+                unpack(c, upto)
 
         ag_own(c)
 
@@ -445,7 +479,7 @@
     cap = (home_win + n - 1) // n
     chunks = ENC_WIN // (2 * PAIRS)
     cols = PAIRS * LANES
-    early = early_positions(n, cap)
+    stages = arrival_stages(n, cap)
 
     hbm = pl.BlockSpec(memory_space=pl.ANY)
     vmem = pl.BlockSpec(memory_space=pltpu.VMEM)
@@ -461,8 +495,10 @@
             pltpu.VMEM(out_weight.shape, BF16),
             pltpu.VMEM((full_width, LANES), F32),
             pltpu.VMEM((n, cap, rows, LANES), BF16),
-            pltpu.VMEM((early, cap, rows, LANES), BF16),
-            pltpu.VMEM((n - early, cap, rows, LANES), BF16),
+            [
+                pltpu.VMEM((high - low, end - first, rows, LANES), BF16)
+                for low, high, first, end in stages
+            ],
             pltpu.VMEM((m, chunks, width, cols), BF16),
             pltpu.VMEM((qkv_weight.shape[1], full_width), BF16),
             pltpu.VMEM((full_width, out_weight.shape[0]), BF16),
@@ -475,7 +511,7 @@
             pltpu.VMEM((ENC_WIN, rows, LANES), BF16),
             pltpu.VMEM((n, cap, rows, LANES), BF16),
             pltpu.VMEM((n + 1, cap, rows, LANES), BF16),
-            dma, dma((2,)), dma((n,)), dma((n,)), dma((n,)), dma((n,)),
+            dma, dma((2,)), dma((len(stages), n)), dma((len(stages), n)), dma((n,)), dma((n,)),
             dma((chunks, m)), dma((chunks, m)), dma((chunks, m)),
             dma((chunks, m)), dma((chunks, m)), dma((chunks, m)),
         ],

time: 103 us -> 99.6 us (0.967)
  Pallas kernels: 97.1 us -> 93.9 us
    pallas_call x1, Pallas kernels: 97.1 us -> 93.9 us  [body(): pl.pallas_call(functools.partial(kernel, n, m, cap), out_shape=jax.ShapeD...]
where the time goes in v6:
time: 99.6 us; the launch traced here: 99.4 us
  Pallas kernels  93.9 us (94%)
  local copies, waits for them, and re-layouts  5.49 us (6%)
    pallas_call x1, Pallas kernels, body(): pl.pallas_call(functools.partial(kernel, n, m, cap), out_shape=jax.ShapeD...  93.9 us
    unnamed x2, local copies, waits for them, and re-layouts  5.49 us

profile of v6, /device:TPU:1, one launch (start us, length us, event | category | flops | bytes accessed | tf_op | source)
XLA Modules:
  0.0 99.4 jit_solution(4112212871925477036)
XLA Ops:
  0.0 2.6 %copy.6 = bf16[4,8,160,128]{3,2,1,0:T(8,128)(2,1)} copy(bf16[4,8,160,128]{3,1,2,0:T(8,128)(2,1)} %bitcast.11) | data formatting | bytes 2621440
  2.6 93.9 %shard_map.55 = bf16[32,160,128]{2,1,0:T(8,128)(2,1)} custom-call(s32[8,32]{1,0:T(8,128)} %plan_ref.1, bf16[32,160,128]{2,1,0:T(8,128)(2,1)} %bitcast.9, f32[10,128]{1,0:T(8,128)} %bitcast.12, bf16[960,1280]{1,0:T(8,128)(2,1)} %bitcast.10, bf16[320,1280]{1,0:T(8,128)(2,1)} %outw_ref.1), custom_call_target="tpu_custom_call" | custom-call | tf_op jit(solution)/shard_map/pallas_call | solution.py:487
  96.5 2.9 %copy.9 = bf16[4,8,160,128]{3,1,2,0:T(8,128)(2,1)} copy(bf16[4,8,160,128]{3,2,1,0:T(8,128)(2,1)} %bitcast.8) | data formatting | bytes 2621440

commit v7 on v6

--- a/solution.py
+++ b/solution.py
@@ -12,6 +12,7 @@
 ENC_WIN = 16
 LANES = 128
 PAIRS = 1
+TILE = 8
 
 LOG2E = 1.4426950408889634
 epsilon = 1e-06
@@ -117,12 +118,13 @@
     n, m, cap,
     plan_ref, x_ref, gain_ref, qkv_ref, outw_ref,
     out_ref,
-    index_v, index_s, outw, gain_t, outb, inbs, gath, qkv_t, outw_t, proj, heads, part, from_left, from_right, total, done, backb, homeb,
+    index_v, index_s, flat, outw, gain_t, outb, inbs, gath, qkv_t, outw_t, proj, heads, part, from_left, from_right, total, done, backb, homeb,
     i_sem, w_sem, d_send, d_recv, b_send, b_recv, ag_recv, ag_right, ag_left, rs_send, rs_left, rs_right,
 ):
     me = lax.axis_index("dp")
     z = lax.axis_index("mp")
-    home_win, rows, _ = x_ref.shape
+    rows = x_ref.shape[1]
+    home_win = x_ref.shape[0] * TILE
     width = 2 * rows
     chunks = gath.shape[1]
     heads_here = qkv_ref.shape[0] // (3 * HEAD_DIM)
@@ -152,10 +154,21 @@
     plan_indices(n, cap, me, plan_ref, index_v)
     load_index = pltpu.make_async_copy(index_v, index_s, i_sem)
     load_index.start()
+
+    def widen(g, _):
+        at = pl.ds(pl.multiple_of(g * (rows * TILE), rows * TILE), rows * TILE)
+        flat[at, :] = x_ref[g].reshape(rows * TILE, LANES).astype(F32)
+        return 0
+
+    lax.fori_loop(0, home_win // TILE, widen, 0)
     load_index.wait()
+
+    def window_rows(s):
+        return pl.ds((s // TILE) * (rows * TILE) + lax.rem(s, TILE), rows, stride=TILE)
+
     for p in range(n):
         for j in range(cap):
-            outb[p, j] = x_ref[index_s[SOURCE, p * cap + j]]
+            outb[p, j] = flat[window_rows(index_s[SOURCE, p * cap + j]), :].astype(BF16)
 
     ends = (z == 0).astype(jnp.int32) + (z == m - 1).astype(jnp.int32)
     pl.semaphore_wait(barrier, n + 1 - ends)
@@ -463,10 +476,17 @@
 
     def place_home(s, _):
         at = index_s[SLOT, s]
-        out_ref[s] = homeb[at // cap, lax.rem(at, cap)]
+        flat[window_rows(s), :] = homeb[at // cap, lax.rem(at, cap)].astype(F32)
         return 0
 
     lax.fori_loop(0, home_win, place_home, 0)
+
+    def narrow(g, _):
+        at = pl.ds(pl.multiple_of(g * (rows * TILE), rows * TILE), rows * TILE)
+        out_ref[g] = flat[at, :].astype(BF16).reshape(rows, TILE, LANES)
+        return 0
+
+    lax.fori_loop(0, home_win // TILE, narrow, 0)
 
 
 def body(patches, norm_gain, qkv_weight, out_weight, window_plan):
@@ -481,17 +501,21 @@
     cols = PAIRS * LANES
     stages = arrival_stages(n, cap)
 
+    tiles = jnp.transpose(
+        patches.reshape(home_win // TILE, TILE, rows, LANES), (0, 2, 1, 3)
+    )
     hbm = pl.BlockSpec(memory_space=pl.ANY)
     vmem = pl.BlockSpec(memory_space=pltpu.VMEM)
     dma = pltpu.SemaphoreType.DMA
     result = pl.pallas_call(
         functools.partial(kernel, n, m, cap),
-        out_shape=jax.ShapeDtypeStruct((home_win, rows, LANES), BF16),
+        out_shape=jax.ShapeDtypeStruct(tiles.shape, BF16),
         in_specs=[vmem] * 3 + [hbm] * 2,
         out_specs=vmem,
         scratch_shapes=[
             pltpu.VMEM((8, LANES), jnp.int32),
             pltpu.SMEM((8, LANES), jnp.int32),
+            pltpu.VMEM((home_win * rows, LANES), F32),
             pltpu.VMEM(out_weight.shape, BF16),
             pltpu.VMEM((full_width, LANES), F32),
             pltpu.VMEM((n, cap, rows, LANES), BF16),
@@ -519,10 +543,10 @@
             collective_id=0, has_side_effects=True, vmem_limit_bytes=56 * 1024 * 1024
         ),
     )(
-        window_plan, patches.reshape(home_win, rows, LANES), norm_gain.reshape(-1, LANES),
+        window_plan, tiles, norm_gain.reshape(-1, LANES),
         qkv_weight.T, out_weight,
     )
-    return result.reshape(home_win, row_width)
+    return jnp.transpose(result, (0, 2, 1, 3)).reshape(home_win, row_width)
 
 
 def solution(mesh):

time: 99.6 us -> 97.2 us (0.976)
  local copies, waits for them, and re-layouts: 5.49 us -> 2.46 us
    unnamed x2 -> x1, local copies, waits for them, and re-layouts: 5.49 us -> 2.46 us
where the time goes in v7:
time: 97.2 us; the launch traced here: 97 us
  Pallas kernels  94.5 us (97%)
  local copies, waits for them, and re-layouts  2.46 us (3%)
    pallas_call x1, Pallas kernels, body(): pl.pallas_call(functools.partial(kernel, n, m, cap), out_shape=jax.ShapeD...  94.5 us
    unnamed x1, local copies, waits for them, and re-layouts  2.46 us

profile of v7, /device:TPU:1, one launch (start us, length us, event | category | flops | bytes accessed | tf_op | source)
XLA Modules:
  0.0 97.0 jit_solution(3471508529370614480)
XLA Ops:
  0.0 94.5 %shard_map.55 = bf16[4,160,8,128]{3,2,1,0:T(8,128)(2,1)} custom-call(s32[8,32]{1,0:T(8,128)} %plan_ref.1, bf16[4,160,8,128]{3,2,1,0:T(8,128)(2,1)} %bitcast.10, f32[10,128]{1,0:T(8,128)} %bitcast.11, bf16[960,1280]{1,0:T(8,128)(2,1)} %bitcast.9, bf16[320,1280]{1,0:T(8,128)(2,1)} %outw_ref.1), custom_call_target="tpu_custom_call" | custom-call | tf_op jit(solution)/shard_map/pallas_call | solution.py:510
  94.5 2.5 %copy.7 = bf16[32,20480]{1,0:T(8,128)(2,1)} copy(bf16[32,20480]{1,0:T(8,128)(2,1)} %bitcast.8) | data formatting | bytes 2621440

commit v8 on v7

--- a/solution.py
+++ b/solution.py
@@ -114,10 +114,14 @@
     index_v[BACK:BACK + 1, :n * cap] = jnp.clip(back, 0, ENC_WIN - 1)
 
 
+def window_rows(s, rows):
+    return pl.ds((s // TILE) * (rows * TILE) + lax.rem(s, TILE), rows, stride=TILE)
+
+
 def kernel(
     n, m, cap,
     plan_ref, x_ref, gain_ref, qkv_ref, outw_ref,
-    out_ref,
+    home_ref, slots_ref,
     index_v, index_s, flat, outw, gain_t, outb, inbs, gath, qkv_t, outw_t, proj, heads, part, from_left, from_right, total, done, backb, homeb,
     i_sem, w_sem, d_send, d_recv, b_send, b_recv, ag_recv, ag_right, ag_left, rs_send, rs_left, rs_right,
 ):
@@ -162,13 +166,9 @@
 
     lax.fori_loop(0, home_win // TILE, widen, 0)
     load_index.wait()
-
-    def window_rows(s):
-        return pl.ds((s // TILE) * (rows * TILE) + lax.rem(s, TILE), rows, stride=TILE)
-
     for p in range(n):
         for j in range(cap):
-            outb[p, j] = flat[window_rows(index_s[SOURCE, p * cap + j]), :].astype(BF16)
+            outb[p, j] = flat[window_rows(index_s[SOURCE, p * cap + j], rows), :].astype(BF16)
 
     ends = (z == 0).astype(jnp.int32) + (z == m - 1).astype(jnp.int32)
     pl.semaphore_wait(barrier, n + 1 - ends)
@@ -474,19 +474,27 @@
     for p in others:
         reply(p).wait()
 
+    home_ref[...] = homeb[...]
+    slots_ref[...] = index_v[...]
+
+
+def place_kernel(slots_ref, home_ref, out_ref, flat):
+    groups, rows = out_ref.shape[:2]
+    cap = home_ref.shape[1]
+
     def place_home(s, _):
-        at = index_s[SLOT, s]
-        flat[window_rows(s), :] = homeb[at // cap, lax.rem(at, cap)].astype(F32)
+        at = slots_ref[SLOT, s]
+        flat[window_rows(s, rows), :] = home_ref[at // cap, lax.rem(at, cap)].astype(F32)
         return 0
 
-    lax.fori_loop(0, home_win, place_home, 0)
+    lax.fori_loop(0, groups * TILE, place_home, 0)
 
     def narrow(g, _):
         at = pl.ds(pl.multiple_of(g * (rows * TILE), rows * TILE), rows * TILE)
         out_ref[g] = flat[at, :].astype(BF16).reshape(rows, TILE, LANES)
         return 0
 
-    lax.fori_loop(0, home_win // TILE, narrow, 0)
+    lax.fori_loop(0, groups, narrow, 0)
 
 
 def body(patches, norm_gain, qkv_weight, out_weight, window_plan):
@@ -507,11 +515,14 @@
     hbm = pl.BlockSpec(memory_space=pl.ANY)
     vmem = pl.BlockSpec(memory_space=pltpu.VMEM)
     dma = pltpu.SemaphoreType.DMA
-    result = pl.pallas_call(
+    answers, index = pl.pallas_call(
         functools.partial(kernel, n, m, cap),
-        out_shape=jax.ShapeDtypeStruct(tiles.shape, BF16),
+        out_shape=[
+            jax.ShapeDtypeStruct((n + 1, cap, rows, LANES), BF16),
+            jax.ShapeDtypeStruct((8, LANES), jnp.int32),
+        ],
         in_specs=[vmem] * 3 + [hbm] * 2,
-        out_specs=vmem,
+        out_specs=[vmem, vmem],
         scratch_shapes=[
             pltpu.VMEM((8, LANES), jnp.int32),
             pltpu.SMEM((8, LANES), jnp.int32),
@@ -546,6 +557,14 @@
         window_plan, tiles, norm_gain.reshape(-1, LANES),
         qkv_weight.T, out_weight,
     )
+    result = pl.pallas_call(
+        place_kernel,
+        out_shape=jax.ShapeDtypeStruct(tiles.shape, BF16),
+        in_specs=[pl.BlockSpec(memory_space=pltpu.SMEM), vmem],
+        out_specs=vmem,
+        scratch_shapes=[pltpu.VMEM((home_win * rows, LANES), F32)],
+        compiler_params=pltpu.CompilerParams(vmem_limit_bytes=24 * 1024 * 1024),
+    )(index, answers)
     return jnp.transpose(result, (0, 2, 1, 3)).reshape(home_win, row_width)
 
 

time: 97.2 us -> 98.7 us (1.015)
  Pallas kernels: 94.5 us -> 96.5 us
    pallas_call x1 -> x2, Pallas kernels: 94.5 us -> 96.5 us  [the longest x1 93.7 us: body(): pl.pallas_call(functools.partial(kernel, n, m, cap), out_shape=[jax.Shape...]
    unnamed x1 -> x4, local copies, waits for them, and re-layouts: 2.46 us -> 2.04 us
where the time goes in v8:
time: 98.7 us; the launch traced here: 98.5 us
  Pallas kernels  96.5 us (98%)
  local copies, waits for them, and re-layouts  2.04 us (2%)
    pallas_call x1, Pallas kernels, body(): pl.pallas_call(functools.partial(kernel, n, m, cap), out_shape=[jax.Shape...  93.7 us
    pallas_call x1, Pallas kernels, body(): pl.pallas_call(place_kernel, out_shape=jax.ShapeDtypeStruct(tiles.shape,...  2.75 us
    unnamed x4, local copies, waits for them, and re-layouts  2.04 us

profile of v8, /device:TPU:1, one launch (start us, length us, event | category | flops | bytes accessed | tf_op | source)
XLA Modules:
  0.0 98.5 jit_solution(10580387969322803359)
XLA Ops:
  0.0 93.7 %shard_map.55 = (bf16[9,4,160,128]{3,2,1,0:T(8,128)(2,1)}, s32[8,128]{1,0:T(8,128)}) custom-call(s32[8,32]{1,0:T(8,128)} %plan_ref.1, bf16[4,160,8,128]{3,2,1,0:T(8,128)(2,1)} %bitcast.9, f32[10,128]{1,0:T(8,128)} %bitcast.10, bf16[960,1280]{1,0:T(8,128)(2,1)} %bitcast.8, bf16[320,1280]{1,0:T(8,128)(2,1)} %outw_ref.1), custom_call_target="tpu_custom_call" | custom-call | tf_op jit(solution)/shard_map/pallas_call | solution.py:518
  93.7 0.0 copy-start
  93.7 1.4 %copy-done = bf16[9,4,160,128]{3,2,1,0:T(8,128)(2,1)S(1)} copy-done((bf16[9,4,160,128]{3,2,1,0:T(8,128)(2,1)S(1)}, bf16[9,4,160,128]{3,2,1,0:T(8,128)(2,1)}, u32[]{:S(2)}) %copy-start) | copy-done | bytes 1474584
  95.1 0.0 copy-start.1
  95.1 0.7 copy-done.1
  95.8 2.8 %shard_map.56 = bf16[4,160,8,128]{3,2,1,0:T(8,128)(2,1)} custom-call(s32[8,128]{1,0:T(8,128)S(1)} %copy-done.1, bf16[9,4,160,128]{3,2,1,0:T(8,128)(2,1)S(1)} %copy-done), custom_call_target="tpu_custom_call" | custom-call | tf_op jit(solution)/shard_map/pallas_call | solution.py:560
Async XLA Ops:
  93.7 1.4 %copy-start = (bf16[9,4,160,128]{3,2,1,0:T(8,128)(2,1)S(1)}, bf16[9,4,160,128]{3,2,1,0:T(8,128)(2,1)}, u32[]{:S(2)}) copy-start(bf16[9,4,160,128]{3,2,1,0:T(8,128)(2,1)} %get-tuple-element.8.home_ref) | copy-start | bytes 4423684
  95.1 0.7 copy-start.1

commit v9 on v7

--- a/solution.py
+++ b/solution.py
@@ -434,8 +434,7 @@
             within(c + m - 1 - t, lambda at, t=t: ag_step(at, t))
         within(c + m - 1, own_chunk)
         within(c, compute)
-        within(c, lambda at: rs_stage(at, 0))
-        for k in range(1, m - 1):
+        for k in range(m - 2, -1, -1):
             within(c - k, lambda at, k=k: rs_stage(at, k))
         within(c - (m - 1), finish)
         return 0

time: 97.2 us -> 97.7 us (level)
  no operation moved by 1% of the time
where the time goes in v9:
time: 97.7 us; the launch traced here: 97.5 us
  Pallas kernels  95.1 us (97%)
  local copies, waits for them, and re-layouts  2.46 us (3%)
    pallas_call x1, Pallas kernels, body(): pl.pallas_call(functools.partial(kernel, n, m, cap), out_shape=jax.ShapeD...  95.1 us
    unnamed x1, local copies, waits for them, and re-layouts  2.46 us

profile of v9, /device:TPU:1, one launch (start us, length us, event | category | flops | bytes accessed | tf_op | source)
XLA Modules:
  0.0 97.5 jit_solution(13906083877726421185)
XLA Ops:
  0.0 95.1 %shard_map.55 = bf16[4,160,8,128]{3,2,1,0:T(8,128)(2,1)} custom-call(s32[8,32]{1,0:T(8,128)} %plan_ref.1, bf16[4,160,8,128]{3,2,1,0:T(8,128)(2,1)} %bitcast.10, f32[10,128]{1,0:T(8,128)} %bitcast.11, bf16[960,1280]{1,0:T(8,128)(2,1)} %bitcast.9, bf16[320,1280]{1,0:T(8,128)(2,1)} %outw_ref.1), custom_call_target="tpu_custom_call" | custom-call | tf_op jit(solution)/shard_map/pallas_call | solution.py:509
  95.1 2.5 %copy.7 = bf16[32,20480]{1,0:T(8,128)(2,1)} copy(bf16[32,20480]{1,0:T(8,128)(2,1)} %bitcast.8) | data formatting | bytes 2621440
